TPU v7x, 32 devices: a whole 2x2x4 slice. The times are simulated.
32 devices in a mesh: table: 4 (over y, x), replica: 8 (over z, core).
Axes of the slice: x: 2, y: 2, z: 4, core: 2. Of those that a mesh axis runs over, the one named last changes fastest.
Arguments:
- embeds: bfloat16 [2048, 512], P('replica', 'table'), may hold values from -6 to 6
- cotangent: bfloat16 [2048, 512], P('replica', 'table'), may hold values from -6 to 6
- send_plan: int32 [8, 4, 8], P('replica'), may hold values from 0 to 7, each once within a row
- work_plan: int32 [8, 4, 8], P('replica', 'table'), may hold values from 0 to 7, each once within a row
- sequence_tiles: int32 [8, 4, 4], P('replica', 'table'), may hold values from 1 to 4, 8 in all within a row
- slopes: float32 [8], replicated, may hold values from 0.002 to 0.2
- uvqk_weight: bfloat16 [512, 2048], replicated, may hold values from -0.25 to 0.25
- out_weight: bfloat16 [512, 512], replicated, may hold values from -0.25 to 0.25
Outputs:
- layer_output: bfloat16 [2048, 512], P('replica', 'table')
- input_gradient: bfloat16 [2048, 512], P('replica', 'table')
Inputs may be any that keep to these rules, and one draw needn't show every extreme that they name: `send_plan`: a device's 8 entries are all different. `work_plan`: a device's 8 entries are all different. `sequence_tiles`: a device's 4 entries sum to 8.
All inputs are finite; a program needn't handle non-finite values.
Results may differ from a plain program's by a relative error of at most 0.013.
Values may be sent and summed in bfloat16 or wider, within the bound.
A program may use at most 64 MiB of HBM per device.

v0:
```python
import jax
import jax.numpy as jnp
from jax import lax
from jax.sharding import PartitionSpec as P

TILE = 8


EPSILON = 1e-05


def layer_norm(features):
    centre = jnp.mean(features, axis=-1, keepdims=True)
    centred = features - centre
    spread = jnp.mean(centred * centred, axis=-1, keepdims=True)
    return centred * lax.rsqrt(spread + EPSILON)


def segment_ids(lengths, row_count, tile_rows):
    boundary = jnp.cumsum(lengths)
    tile_index = jnp.arange(row_count, dtype=jnp.int32) // tile_rows
    return jnp.sum((tile_index[None, :] >= boundary[:, None]).astype(jnp.int32), axis=0)


def hstu_layer(inputs, segment, slopes, uvqk_weight, out_weight):
    row_count, feature_count = inputs.shape
    head_count = slopes.shape[0]
    head_size = feature_count // head_count
    score_scale = head_size ** (-0.5)
    normed = layer_norm(inputs.astype(jnp.float32)).astype(jnp.bfloat16)
    projected = jax.nn.silu(jnp.dot(normed, uvqk_weight, preferred_element_type=jnp.float32))
    gate_part = projected[:, :feature_count]
    value_part = projected[:, feature_count : 2 * feature_count].astype(jnp.bfloat16)
    query_part = projected[:, 2 * feature_count : 3 * feature_count].astype(jnp.bfloat16)
    key_part = projected[:, 3 * feature_count :].astype(jnp.bfloat16)
    row_index = lax.broadcasted_iota(jnp.int32, (row_count, row_count), 0)
    col_index = lax.broadcasted_iota(jnp.int32, (row_count, row_count), 1)
    allowed = (segment[:, None] == segment[None, :]) & (col_index <= row_index)
    distance = (row_index - col_index).astype(jnp.float32)
    pieces = []
    for head_index in range(head_count):
        lower = head_index * head_size
        upper = lower + head_size
        scores = jnp.dot(
            query_part[:, lower:upper],
            key_part[:, lower:upper].T,
            preferred_element_type=jnp.float32,
        )
        scores = scores * score_scale - slopes[head_index] * distance
        weights = jnp.where(allowed, jax.nn.silu(scores), jnp.zeros_like(scores)).astype(
            jnp.bfloat16
        )
        pieces.append(
            jnp.dot(weights, value_part[:, lower:upper], preferred_element_type=jnp.float32)
        )
    attended = jnp.concatenate(pieces, axis=1)
    gated = (layer_norm(attended) * gate_part).astype(jnp.bfloat16)
    mixing = jnp.dot(gated, out_weight, preferred_element_type=jnp.float32)
    return (inputs.astype(jnp.float32) + mixing).astype(jnp.bfloat16)


def forward_backward(inputs, grad_rows, segment, slopes, uvqk_weight, out_weight):

    def apply_layer(layer_input):
        return hstu_layer(layer_input, segment, slopes, uvqk_weight, out_weight)

    outputs, pullback = jax.vjp(apply_layer, inputs)
    return (outputs, pullback(grad_rows)[0])


def shards(
    embeds, cotangent, send_plan, work_plan, sequence_tiles, slopes, uvqk_weight, out_weight
):
    table_count = lax.axis_size("table")
    replica_count = lax.axis_size("replica")
    column_count = embeds.shape[1]
    row_count = embeds.shape[0] // table_count
    tile_count = row_count // TILE
    peer_rows = row_count // replica_count
    feature_count = column_count * table_count
    block_plans = send_plan[0]
    own_send = lax.dynamic_index_in_dim(block_plans, lax.axis_index("table"), 0, keepdims=False)
    own_work = work_plan[0, 0]
    segment = segment_ids(sequence_tiles[0, 0], row_count, TILE)
    tile_order = jnp.arange(tile_count, dtype=jnp.int32)
    row_inputs, row_grads = (
        lax.all_to_all(embeds, "table", split_axis=0, concat_axis=1, tiled=True),
        lax.all_to_all(cotangent, "table", split_axis=0, concat_axis=1, tiled=True),
    )

    def to_slots(shard_rows):
        tiled = shard_rows.reshape(tile_count, TILE, feature_count)
        return tiled[own_send]

    got_inputs, got_grads = (
        lax.all_to_all(to_slots(row_inputs), "replica", split_axis=0, concat_axis=0, tiled=True),
        lax.all_to_all(to_slots(row_grads), "replica", split_axis=0, concat_axis=0, tiled=True),
    )
    work_inputs = got_inputs[own_work].reshape(row_count, feature_count)
    work_grads = got_grads[own_work].reshape(row_count, feature_count)
    outputs, gradient = forward_backward(
        work_inputs, work_grads, segment, slopes, uvqk_weight, out_weight
    )
    undo_work = jnp.zeros((tile_count,), jnp.int32).at[own_work].set(tile_order)

    def to_sources(result):
        return result.reshape(tile_count, TILE, feature_count)[undo_work]

    slot_outputs = to_sources(outputs)
    slot_grads = to_sources(gradient)
    back_outputs, back_grads = (
        lax.all_to_all(slot_outputs, "replica", split_axis=0, concat_axis=0, tiled=True),
        lax.all_to_all(slot_grads, "replica", split_axis=0, concat_axis=0, tiled=True),
    )
    undo_send = jnp.zeros((tile_count,), jnp.int32).at[own_send].set(tile_order)

    def to_home(result):
        return result[undo_send].reshape(row_count, feature_count)

    layer_output, input_gradient = (
        lax.all_to_all(to_home(back_outputs), "table", split_axis=1, concat_axis=0, tiled=True),
        lax.all_to_all(to_home(back_grads), "table", split_axis=1, concat_axis=0, tiled=True),
    )
    return (layer_output, input_gradient)


def solution(mesh):
    in_specs = (
        P("replica", "table"),
        P("replica", "table"),
        P("replica", None, None),
        P("replica", "table", None),
        P("replica", "table", None),
        P(),
        P(),
        P(),
    )
    out_specs = (P("replica", "table"), P("replica", "table"))
    return jax.shard_map(shards, mesh=mesh, in_specs=in_specs, out_specs=out_specs, check_vma=False)
```

profile of v0, /device:TPU:0, one launch (start us, length us, event | category | flops | bytes accessed | tf_op | source)
XLA Modules:
  0.0 99.8 jit_solution(6266185767778423695)
XLA Ops:
  0.6 5.3 %all-to-all-start = ((bf16[4,64,128]{2,1,0:T(8,128)(2,1)}), bf16[4,64,128]{2,1,0:T(8,128)(2,1)S(1)}, u32[]{:S(2)}, u32[]{:S(2)}) async-start(bf16[4,64,128]{2,1,0:T(8,128)(2,1)} %bitcast.89), calls=%async_computation | async-start | bytes 131072 | tf_op jit(solution)/shard_map/all_to_all | solution.py:87
  7.3 1.6 %fusion.173 = (f32[1]{0:T(128)}, f32[1]{0:T(128)}, f32[1]{0:T(128)}, f32[1]{0:T(128)}, f32[1]{0:T(128)}, /*index=5*/f32[1]{0:T(128)}, f32[1]{0:T(128)}, f32[1]{0:T(128)}) fusion(f32[8]{0:T(128)} %param.13), kind=kLoop, calls=%fused_computation.287 | loop fusion | bytes 64 | tf_op jit(solution)/shard_map/jvp()/slice | solution.py:49
  9.6 1.2 %all-to-all-done = bf16[4,64,128]{2,1,0:T(8,128)(2,1)S(1)} async-done(((bf16[4,64,128]{2,1,0:T(8,128)(2,1)}), bf16[4,64,128]{2,1,0:T(8,128)(2,1)S(1)}, u32[]{:S(2)}, u32[]{:S(2)}) %all-to-all-start) | async-done | bytes 65568 | tf_op jit(solution)/shard_map/all_to_all | solution.py:87
  10.8 3.3 %all-to-all-start.4 = ((bf16[4,64,128]{2,1,0:T(8,128)(2,1)}), bf16[4,64,128]{2,1,0:T(8,128)(2,1)S(1)}, u32[]{:S(2)}, u32[]{:S(2)}) async-start(bf16[4,64,128]{2,1,0:T(8,128)(2,1)} %bitcast.90), calls=%async_computation.4 | async-start | bytes 131072 | tf_op jit(solution)/shard_map/all_to_all | solution.py:88
  14.2 1.2 %gather_fusion = bf16[8,8,512]{2,1,0:T(8,128)(2,1)} fusion(bf16[8,8,512]{2,1,0:T(8,128)(2,1)S(1)} %reshape.225, s32[1024]{0:T(1024)S(1)} %pad_clamp_fusion.3), kind=kCustom, calls=%fused_computation | custom fusion | bytes 131104 | tf_op jit(solution)/shard_map/gather | solution.py:93
  15.4 3.5 %all-to-all-done.4 = bf16[4,64,128]{2,1,0:T(8,128)(2,1)S(1)} async-done(((bf16[4,64,128]{2,1,0:T(8,128)(2,1)}), bf16[4,64,128]{2,1,0:T(8,128)(2,1)S(1)}, u32[]{:S(2)}, u32[]{:S(2)}) %all-to-all-start.4) | async-done | bytes 65568 | tf_op jit(solution)/shard_map/all_to_all | solution.py:88
  18.9 4.9 %all-to-all-start.1 = ((bf16[8,8,512]{2,1,0:T(8,128)(2,1)}), bf16[8,8,512]{2,1,0:T(8,128)(2,1)S(1)}, u32[]{:S(2)}, u32[]{:S(2)}) async-start(bf16[8,8,512]{2,1,0:T(8,128)(2,1)} %gather_fusion), calls=%async_computation.1 | async-start | bytes 131072 | tf_op jit(solution)/shard_map/all_to_all | solution.py:96
  24.6 1.1 %scatter_custom_fusion.1 = s32[8]{0:T(128)} fusion(s32[8]{0:T(128)S(1)} %fusion.159, s32[8]{0:T(128)S(1)} %iota.58, s32[]{:T(128)} %constant.64.clone.1), kind=kCustom, calls=%fused_computation.276 | custom fusion | bytes 36 | tf_op jit(solution)/shard_map/scatter | solution.py:115
  25.9 1.2 %gather_fusion.4 = bf16[8,8,512]{2,1,0:T(8,128)(2,1)} fusion(bf16[8,8,512]{2,1,0:T(8,128)(2,1)S(1)} %reshape.229, s32[1024]{0:T(1024)S(1)} %pad_clamp_fusion.3), kind=kCustom, calls=%fused_computation.4 | custom fusion | bytes 131104 | tf_op jit(solution)/shard_map/gather | solution.py:93
  27.1 2.6 %all-to-all-done.1 = bf16[8,8,512]{2,1,0:T(8,128)(2,1)S(1)} async-done(((bf16[8,8,512]{2,1,0:T(8,128)(2,1)}), bf16[8,8,512]{2,1,0:T(8,128)(2,1)S(1)}, u32[]{:S(2)}, u32[]{:S(2)}) %all-to-all-start.1) | async-done | bytes 65568 | tf_op jit(solution)/shard_map/all_to_all | solution.py:96
  29.7 3.4 %all-to-all-start.5 = ((bf16[8,8,512]{2,1,0:T(8,128)(2,1)}), bf16[8,8,512]{2,1,0:T(8,128)(2,1)S(1)}, u32[]{:S(2)}, u32[]{:S(2)}) async-start(bf16[8,8,512]{2,1,0:T(8,128)(2,1)} %gather_fusion.4), calls=%async_computation.5 | async-start | bytes 131072 | tf_op jit(solution)/shard_map/all_to_all | solution.py:97
  34.1 1.5 %fusion.171 = (bf16[64,2048]{1,0:T(8,128)(2,1)S(1)}, f32[64,2048]{1,0:T(8,128)}, f32[64,2048]{1,0:T(8,128)}) fusion(bf16[512,2048]{1,0:T(8,128)(2,1)S(1)} %copy-done, bf16[8,8,512]{2,1,0:T(8,128)(2,1)S(1)} %gather_fusion.1, f32[64]{0:T(128)S(1)} %rsqrt.20, f32[64]{0:T(128)S(1)} %div.78), kind=kOutput, calls=%fused_computation.286 | convolution fusion | flops 135004160 | bytes 3473920 | tf_op jit(solution)/shard_map/jvp()/dot_general | solution.py:31
  35.6 0.9 fusion.4
  38.9 0.8 fusion.8
  43.5 0.8 fusion.181
  45.2 0.9 fusion.178
  46.9 0.9 fusion.176
  47.8 0.8 fusion.175
  50.9 1.3 %multiply_reduce_fusion = (f32[64]{0:T(128)S(1)}, f32[64]{0:T(128)S(1)}, f32[64,512]{1,0:T(8,128)S(1)}) fusion(f32[64,512]{1,0:T(8,128)S(1)} %concatenate.3, f32[64]{0:T(128)S(1)} %add_multiply_fusion, f32[64,2048]{1,0:T(8,128)} %get-tuple-element.7, bf16[512,512]{1,0:T(8,128)(2,1)S(1)} %copy-done.1, bf16[8,8,512]{2,1,0:T(8,128)(2,1)S(1)} %gather_fusion.5), kind=kOutput, calls=%fused_computation.113 | convolution fusion | flops 33816448 | bytes 983808 | tf_op jit(solution)/shard_map/transpose(jvp())/dot_general | solution.py:58
  52.3 1.2 %fusion.3 = bf16[8,8,512]{2,1,0:T(8,128)(2,1)S(1)} fusion(bf16[512,512]{1,0:T(8,128)(2,1)S(1)} %copy-done.1, bf16[8,8,512]{2,1,0:T(8,128)(2,1)S(1)} %gather_fusion.1, f32[64,2048]{1,0:T(8,128)} %get-tuple-element.7, f32[64,512]{1,0:T(8,128)S(1)} %concatenate.3, f32[64]{0:T(128)S(1)} %get-tuple-element.10, f32[64]{0:T(128)S(1)} %add_multiply_fusion), kind=kOutput, calls=%fused_computation.16 | convolution fusion | flops 33783808 | bytes 918016 | tf_op jit(solution)/shard_map/jvp()/dot_general | solution.py:58
  53.4 1.1 %fusion.170 = (f32[64]{0:T(128)S(1)}, f32[64,512]{1,0:T(8,128)S(1)}, f32[64,512]{1,0:T(8,128)S(1)}) fusion(f32[64]{0:T(128)S(1)} %get-tuple-element.9, f32[64,512]{1,0:T(8,128)S(1)} %concatenate.3, f32[64]{0:T(128)S(1)} %add_multiply_fusion, f32[64]{0:T(128)S(1)} %get-tuple-element.10, f32[64,512]{1,0:T(8,128)S(1)} %get-tuple-element.36, ...), kind=kLoop, calls=%fused_computation.285 | loop fusion | flops 294848 | bytes 656384 | tf_op jit(solution)/shard_map/transpose(jvp())/reduce_sum | solution.py:14
  61.0 1.2 %gather_fusion.2 = bf16[8,8,512]{2,1,0:T(8,128)(2,1)} fusion(bf16[8,8,512]{2,1,0:T(8,128)(2,1)S(1)} %fusion.3, s32[1024]{0:T(1024)S(1)} %pad_clamp_fusion.1), kind=kCustom, calls=%fused_computation.2 | custom fusion | bytes 131104 | tf_op jit(solution)/shard_map/gather | solution.py:107
  62.2 5.0 %all-to-all-start.2 = ((bf16[8,8,512]{2,1,0:T(8,128)(2,1)}), bf16[8,8,512]{2,1,0:T(8,128)(2,1)S(1)}, u32[]{:S(2)}, u32[]{:S(2)}) async-start(bf16[8,8,512]{2,1,0:T(8,128)(2,1)} %gather_fusion.2), calls=%async_computation.2 | async-start | bytes 131072 | tf_op jit(solution)/shard_map/all_to_all | solution.py:112
  67.5 1.9 %fusion.50 = (f32[64]{0:T(128)S(1)}, f32[64,512]{1,0:T(8,128)S(1)}) fusion(bf16[8,8,512]{2,1,0:T(8,128)(2,1)S(1)} %gather_fusion.1, f32[64]{0:T(128)S(1)} %div.78, bf16[512,2048]{1,0:T(8,128)(2,1)S(1)} %copy-done, f32[64,2048]{1,0:T(8,128)} %get-tuple-element.19, f32[64,512]{1,0:T(8,128)S(1)} %get-tuple-element.8, ...), kind=kOutput, calls=%fused_computation.109 | convolution fusion | flops 136380352 | bytes 3146240 | tf_op jit(solution)/shard_map/transpose(jvp())/dot_general | solution.py:31
  69.7 1.2 %gather_fusion.6 = bf16[8,8,512]{2,1,0:T(8,128)(2,1)} fusion(bf16[8,8,512]{2,1,0:T(8,128)(2,1)S(1)} %fusion.54, s32[1024]{0:T(1024)S(1)} %pad_clamp_fusion.1), kind=kCustom, calls=%fused_computation.6 | custom fusion | bytes 131104 | tf_op jit(solution)/shard_map/gather | solution.py:107
  70.9 2.2 %all-to-all-done.2 = bf16[8,8,512]{2,1,0:T(8,128)(2,1)S(1)} async-done(((bf16[8,8,512]{2,1,0:T(8,128)(2,1)}), bf16[8,8,512]{2,1,0:T(8,128)(2,1)S(1)}, u32[]{:S(2)}, u32[]{:S(2)}) %all-to-all-start.2) | async-done | bytes 65568 | tf_op jit(solution)/shard_map/all_to_all | solution.py:112
  73.1 3.4 %all-to-all-start.6 = ((bf16[8,8,512]{2,1,0:T(8,128)(2,1)}), bf16[8,8,512]{2,1,0:T(8,128)(2,1)S(1)}, u32[]{:S(2)}, u32[]{:S(2)}) async-start(bf16[8,8,512]{2,1,0:T(8,128)(2,1)} %gather_fusion.6), calls=%async_computation.6 | async-start | bytes 131072 | tf_op jit(solution)/shard_map/all_to_all | solution.py:113
  77.7 4.6 %all-to-all-done.6 = bf16[8,8,512]{2,1,0:T(8,128)(2,1)S(1)} async-done(((bf16[8,8,512]{2,1,0:T(8,128)(2,1)}), bf16[8,8,512]{2,1,0:T(8,128)(2,1)S(1)}, u32[]{:S(2)}, u32[]{:S(2)}) %all-to-all-start.6) | async-done | bytes 65568 | tf_op jit(solution)/shard_map/all_to_all | solution.py:113
  82.3 3.3 %all-to-all-start.3 = ((bf16[64,4,128]{2,0,1:T(8,128)(2,1)}), bf16[64,4,128]{2,0,1:T(8,128)(2,1)S(1)}, u32[]{:S(2)}, u32[]{:S(2)}) async-start(bf16[64,4,128]{2,0,1:T(8,128)(2,1)} %copy.21), calls=%async_computation.3 | async-start | bytes 131072 | tf_op jit(solution)/shard_map/all_to_all | solution.py:121
  86.8 3.6 %all-to-all-done.3 = bf16[64,4,128]{2,0,1:T(8,128)(2,1)S(1)} async-done(((bf16[64,4,128]{2,0,1:T(8,128)(2,1)}), bf16[64,4,128]{2,0,1:T(8,128)(2,1)S(1)}, u32[]{:S(2)}, u32[]{:S(2)}) %all-to-all-start.3) | async-done | bytes 65568 | tf_op jit(solution)/shard_map/all_to_all | solution.py:121
  90.4 3.3 %all-to-all-start.7 = ((bf16[64,4,128]{2,0,1:T(8,128)(2,1)}), bf16[64,4,128]{2,0,1:T(8,128)(2,1)S(1)}, u32[]{:S(2)}, u32[]{:S(2)}) async-start(bf16[64,4,128]{2,0,1:T(8,128)(2,1)} %copy.23), calls=%async_computation.7 | async-start | bytes 131072 | tf_op jit(solution)/shard_map/all_to_all | solution.py:122
  93.7 4.8 %all-to-all-done.7 = bf16[64,4,128]{2,0,1:T(8,128)(2,1)S(1)} async-done(((bf16[64,4,128]{2,0,1:T(8,128)(2,1)}), bf16[64,4,128]{2,0,1:T(8,128)(2,1)S(1)}, u32[]{:S(2)}, u32[]{:S(2)}) %all-to-all-start.7) | async-done | bytes 65568 | tf_op jit(solution)/shard_map/all_to_all | solution.py:122
  (123 shorter events, 24.6 us)
Async XLA Ops:
  0.6 33.4 %copy-start = (bf16[512,2048]{1,0:T(8,128)(2,1)S(1)}, bf16[512,2048]{1,0:T(8,128)(2,1)}, u32[]{:S(2)}) copy-start(bf16[512,2048]{1,0:T(8,128)(2,1)} %param.14) | copy-start | bytes 6291460
  0.6 10.2 %all-to-all-start = ((bf16[4,64,128]{2,1,0:T(8,128)(2,1)}), bf16[4,64,128]{2,1,0:T(8,128)(2,1)S(1)}, u32[]{:S(2)}, u32[]{:S(2)}) async-start(bf16[4,64,128]{2,1,0:T(8,128)(2,1)} %bitcast.89), calls=%async_computation | async-start | bytes 131072 | tf_op jit(solution)/shard_map/all_to_all | solution.py:87
  10.8 8.1 %all-to-all-start.4 = ((bf16[4,64,128]{2,1,0:T(8,128)(2,1)}), bf16[4,64,128]{2,1,0:T(8,128)(2,1)S(1)}, u32[]{:S(2)}, u32[]{:S(2)}) async-start(bf16[4,64,128]{2,1,0:T(8,128)(2,1)} %bitcast.90), calls=%async_computation.4 | async-start | bytes 131072 | tf_op jit(solution)/shard_map/all_to_all | solution.py:88
  18.9 10.8 %all-to-all-start.1 = ((bf16[8,8,512]{2,1,0:T(8,128)(2,1)}), bf16[8,8,512]{2,1,0:T(8,128)(2,1)S(1)}, u32[]{:S(2)}, u32[]{:S(2)}) async-start(bf16[8,8,512]{2,1,0:T(8,128)(2,1)} %gather_fusion), calls=%async_computation.1 | async-start | bytes 131072 | tf_op jit(solution)/shard_map/all_to_all | solution.py:96
  25.9 22.8 %copy-start.14 = (s32[64]{0:T(128)}, s32[64]{0:T(128)S(1)}, u32[]{:S(2)}) copy-start(s32[64]{0:T(128)S(1)} %convert_reduce_fusion.1) | copy-start | bytes 772
  29.7 20.6 %all-to-all-start.5 = ((bf16[8,8,512]{2,1,0:T(8,128)(2,1)}), bf16[8,8,512]{2,1,0:T(8,128)(2,1)S(1)}, u32[]{:S(2)}, u32[]{:S(2)}) async-start(bf16[8,8,512]{2,1,0:T(8,128)(2,1)} %gather_fusion.4), calls=%async_computation.5 | async-start | bytes 131072 | tf_op jit(solution)/shard_map/all_to_all | solution.py:97
  34.0 6.5 %copy-start.12 = (f32[64]{0:T(128)}, f32[64]{0:T(128)S(1)}, u32[]{:S(2)}) copy-start(f32[64]{0:T(128)S(1)} %add.156) | copy-start | bytes 772
  34.1 6.5 %copy-start.10 = (f32[64]{0:T(128)}, f32[64]{0:T(128)S(1)}, u32[]{:S(2)}) copy-start(f32[64]{0:T(128)S(1)} %rsqrt.20) | copy-start | bytes 772
  35.6 15.3 %copy-start.1 = (bf16[512,512]{1,0:T(8,128)(2,1)S(1)}, bf16[512,512]{1,0:T(8,128)(2,1)}, u32[]{:S(2)}) copy-start(bf16[512,512]{1,0:T(8,128)(2,1)} %param.15) | copy-start | bytes 1572868
  39.7 9.8 %copy-start.2 = (f32[64,64]{1,0:T(8,128)}, f32[64,64]{1,0:T(8,128)S(1)}, u32[]{:S(2)}) copy-start(f32[64,64]{1,0:T(8,128)S(1)} %fusion.8) | copy-start | bytes 49156
  40.5 3.8 %copy-start.4 = (f32[64,64]{1,0:T(8,128)}, f32[64,64]{1,0:T(8,128)S(1)}, u32[]{:S(2)}) copy-start(f32[64,64]{1,0:T(8,128)S(1)} %fusion.9) | copy-start | bytes 49156
  41.3 2.2 %copy-start.6 = (f32[64,64]{1,0:T(8,128)}, f32[64,64]{1,0:T(8,128)S(1)}, u32[]{:S(2)}) copy-start(f32[64,64]{1,0:T(8,128)S(1)} %fusion.10) | copy-start | bytes 49156
  42.1 0.6 copy-start.8
  49.6 5.1 %copy-start.9 = (f32[64,64]{1,0:T(8,128)S(1)}, f32[64,64]{1,0:T(8,128)}, u32[]{:S(2)}) copy-start(f32[64,64]{1,0:T(8,128)} %copy-done.8) | copy-start | bytes 49156
  49.6 5.5 %copy-start.7 = (f32[64,64]{1,0:T(8,128)S(1)}, f32[64,64]{1,0:T(8,128)}, u32[]{:S(2)}) copy-start(f32[64,64]{1,0:T(8,128)} %copy-done.6) | copy-start | bytes 49156
  49.6 5.9 %copy-start.5 = (f32[64,64]{1,0:T(8,128)S(1)}, f32[64,64]{1,0:T(8,128)}, u32[]{:S(2)}) copy-start(f32[64,64]{1,0:T(8,128)} %copy-done.4) | copy-start | bytes 49156
  50.9 3.8 %copy-start.15 = (s32[64]{0:T(128)S(1)}, s32[64]{0:T(128)}, u32[]{:S(2)}) copy-start(s32[64]{0:T(128)} %copy-done.14) | copy-start | bytes 772
  50.9 5.0 %copy-start.3 = (f32[64,64]{1,0:T(8,128)S(1)}, f32[64,64]{1,0:T(8,128)}, u32[]{:S(2)}) copy-start(f32[64,64]{1,0:T(8,128)} %copy-done.2) | copy-start | bytes 49156
  62.2 10.9 %all-to-all-start.2 = ((bf16[8,8,512]{2,1,0:T(8,128)(2,1)}), bf16[8,8,512]{2,1,0:T(8,128)(2,1)S(1)}, u32[]{:S(2)}, u32[]{:S(2)}) async-start(bf16[8,8,512]{2,1,0:T(8,128)(2,1)} %gather_fusion.2), calls=%async_computation.2 | async-start | bytes 131072 | tf_op jit(solution)/shard_map/all_to_all | solution.py:112
  67.4 2.0 %copy-start.13 = (f32[64]{0:T(128)S(1)}, f32[64]{0:T(128)}, u32[]{:S(2)}) copy-start(f32[64]{0:T(128)} %copy-done.12) | copy-start | bytes 772
  67.4 2.0 %copy-start.11 = (f32[64]{0:T(128)S(1)}, f32[64]{0:T(128)}, u32[]{:S(2)}) copy-start(f32[64]{0:T(128)} %copy-done.10) | copy-start | bytes 772
  67.5 9.0 %copy-start.16 = (s32[8]{0:T(128)S(1)}, s32[8]{0:T(128)}, u32[]{:S(2)}) copy-start(s32[8]{0:T(128)} %scatter_custom_fusion.1) | copy-start | bytes 100
  73.1 9.2 %all-to-all-start.6 = ((bf16[8,8,512]{2,1,0:T(8,128)(2,1)}), bf16[8,8,512]{2,1,0:T(8,128)(2,1)S(1)}, u32[]{:S(2)}, u32[]{:S(2)}) async-start(bf16[8,8,512]{2,1,0:T(8,128)(2,1)} %gather_fusion.6), calls=%async_computation.6 | async-start | bytes 131072 | tf_op jit(solution)/shard_map/all_to_all | solution.py:113
  82.3 8.1 %all-to-all-start.3 = ((bf16[64,4,128]{2,0,1:T(8,128)(2,1)}), bf16[64,4,128]{2,0,1:T(8,128)(2,1)S(1)}, u32[]{:S(2)}, u32[]{:S(2)}) async-start(bf16[64,4,128]{2,0,1:T(8,128)(2,1)} %copy.21), calls=%async_computation.3 | async-start | bytes 131072 | tf_op jit(solution)/shard_map/all_to_all | solution.py:121
  90.4 8.1 %all-to-all-start.7 = ((bf16[64,4,128]{2,0,1:T(8,128)(2,1)}), bf16[64,4,128]{2,0,1:T(8,128)(2,1)S(1)}, u32[]{:S(2)}, u32[]{:S(2)}) async-start(bf16[64,4,128]{2,0,1:T(8,128)(2,1)} %copy.23), calls=%async_computation.7 | async-start | bytes 131072 | tf_op jit(solution)/shard_map/all_to_all | solution.py:122
where the time goes:
time: 101 us; the launch traced here: 99.8 us
  starting transfers between devices  31.8 us (31%)
  matrix products  25.3 us (25%)
  waiting for transfers between devices  22.5 us (22%)
  local copies, waits for them, and re-layouts  14 us (14%)
  other arithmetic  5.07 us (5%)
  between operations  1.13 us (1%)
    dot_general x24, matrix products, hstu_layer(): jnp.dot(weights, value_part[:, lower:upper], preferred_element_type=jnp.f...  10.2 us
    dot_general x24, matrix products, hstu_layer(): jnp.dot(query_part[:, lower:upper], key_part[:, lower:upper].T, preferred...  9.24 us
    all_to_all x1, starting transfers between devices, shards(): lax.all_to_all(embeds, 'table', split_axis=0, concat_axis=1, tiled=True)  5.31 us
    all_to_all x1, starting transfers between devices, shards(): lax.all_to_all(slot_outputs, 'replica', split_axis=0, concat_axis=0, tile...  5.03 us
    all_to_all x1, starting transfers between devices, shards(): lax.all_to_all(to_slots(row_inputs), 'replica', split_axis=0, concat_axis...  4.88 us
    all_to_all x1, waiting for transfers between devices, shards(): lax.all_to_all(to_home(back_grads), 'table', split_axis=1, concat_axis=0,...  4.81 us
    all_to_all x1, waiting for transfers between devices, shards(): lax.all_to_all(slot_grads, 'replica', split_axis=0, concat_axis=0, tiled=...  4.59 us
    all_to_all x1, waiting for transfers between devices, shards(): lax.all_to_all(to_home(back_outputs), 'table', split_axis=1, concat_axis=...  3.59 us
  transfers between devices with their start and end apart: 8, of which 7 were waited for; matrix products, arithmetic and copies ran while one was open for 31% of the time, Pallas kernels for 0%

commit v1 on v0

--- a/solution.py
+++ b/solution.py
@@ -1,7 +1,17 @@
+import functools
+
 import jax
 import jax.numpy as jnp
 from jax import lax
+from jax.experimental import pallas as pl
+from jax.experimental.pallas import tpu as pltpu
 from jax.sharding import PartitionSpec as P
+
+MESH = pl.DeviceIdType.MESH
+MXU = 256
+LANES = 128
+F32 = jnp.float32
+BF16 = jnp.bfloat16
 
 TILE = 8
 
@@ -124,6 +134,291 @@
     return (layer_output, input_gradient)
 
 
+NT = (((1,), (1,)), ((), ()))
+TN = (((0,), (0,)), ((), ()))
+
+
+def mm(a, b, dims=(((1,), (0,)), ((), ()))):
+    return lax.dot_general(a, b, dims, preferred_element_type=F32)
+
+
+def norm_parts(features):
+    centred = features - jnp.mean(features, axis=-1, keepdims=True)
+    scale = lax.rsqrt(jnp.mean(centred * centred, axis=-1, keepdims=True) + EPSILON)
+    return centred * scale, scale
+
+
+def norm_back(grad, normal, scale):
+    along = jnp.mean(grad * normal, axis=-1, keepdims=True)
+    return scale * (grad - jnp.mean(grad, axis=-1, keepdims=True) - normal * along)
+
+
+def silu_parts(v):
+    sig = 0.5 * jnp.tanh(0.5 * v) + 0.5
+    value = v * sig
+    return value, sig + value * (1.0 - sig)
+
+
+def fused_kernel(
+    T, R, H,
+    send_ref, work_ref, seq_ref, slope_ref, emb_ref, cot_ref, wu_hbm, wo_hbm,
+    out_ref, grad_ref,
+    wu, wo, emb32, cot32, stage, got, x_s, dy_s, slope_s, back, ret, inv,
+    w_sem, send_sem, recv_sem, send_sem2, recv_sem2,
+):
+    n = T * R
+    rows = R * TILE
+    width = emb_ref.shape[1]
+    feat = T * width
+    hs = feat // H
+    G = max(1, min(H, MXU // max(hs, rows)))
+    gw, gr = G * hs, G * rows
+    scale = hs ** (-0.5)
+    me_t = lax.axis_index("table")
+    me_r = lax.axis_index("replica")
+    me = me_r * T + me_t
+
+    wu_copy = pltpu.make_async_copy(wu_hbm, wu, w_sem.at[0])
+    wo_copy = pltpu.make_async_copy(wo_hbm, wo, w_sem.at[1])
+    wu_copy.start()
+    wo_copy.start()
+
+    def peer(off):
+        other = lax.rem(me + off, n)
+        return other, {"table": lax.rem(other, T), "replica": other // T}
+
+    barrier = pltpu.get_barrier_semaphore()
+
+    def greet(off, carry):
+        pl.semaphore_signal(barrier, inc=1, device_id=peer(off)[1], device_id_type=MESH)
+        return carry
+
+    lax.fori_loop(1, n, greet, 0)
+
+    emb32[...] = emb_ref[...].astype(F32).reshape(emb32.shape)
+    cot32[...] = cot_ref[...].astype(F32).reshape(cot32.shape)
+    for d in range(R):
+        for t in range(T):
+            k = t * R + send_ref[0, t, d]
+            stage[d * T + t] = jnp.concatenate([emb32[k], cot32[k]], axis=0).astype(BF16)
+
+    pl.semaphore_wait(barrier, n - 1)
+
+    def post(src, dst, s_sem, r_sem):
+        def one(off, carry):
+            other, device = peer(off)
+            pltpu.make_async_remote_copy(
+                src_ref=src.at[other],
+                dst_ref=dst.at[me],
+                send_sem=s_sem,
+                recv_sem=r_sem,
+                device_id=device,
+                device_id_type=MESH,
+            ).start()
+            return carry
+
+        lax.fori_loop(1, n, one, 0)
+        dst[me] = src[me]
+
+    def settle(ref, sem):
+        part = ref.at[pl.ds(0, n - 1)]
+        pltpu.make_async_copy(part, part, sem).wait()
+
+    post(stage, got, send_sem, recv_sem)
+
+    for t in range(T):
+        for j in range(R):
+            found = jnp.int32(0)
+            for d in range(1, R):
+                found = jnp.where(send_ref[0, t, d] == j, d, found)
+            inv[t, j] = found
+
+    bounds = []
+    total = jnp.int32(0)
+    for j in range(seq_ref.shape[2]):
+        total = total + seq_ref[0, 0, j]
+        bounds.append(total)
+
+    def places(index):
+        slot = index // TILE
+        place = jnp.zeros_like(index)
+        for w in range(1, R):
+            place = jnp.where(slot == work_ref[0, 0, w], w, place)
+        segment = jnp.zeros_like(index)
+        for bound in bounds:
+            segment = segment + (place >= bound).astype(jnp.int32)
+        return place * TILE + index % TILE, segment
+
+    row_pos, row_seg = places(lax.broadcasted_iota(jnp.int32, (rows, 1), 0))
+    lane = lax.broadcasted_iota(jnp.int32, (1, gr), 1)
+    col_pos, col_seg = places(lane % rows)
+    distance = (row_pos - col_pos).astype(F32)
+    allowed = (row_seg == col_seg) & (col_pos <= row_pos)
+    slope_s[...] = jnp.where(allowed, distance, -1.0)
+    same_head = (
+        lax.broadcasted_iota(jnp.int32, (gr, gw), 0) // rows
+        == lax.broadcasted_iota(jnp.int32, (gr, gw), 1) // hs
+    )
+    head_mask = jnp.where(same_head, 1.0, 0.0)
+    head_mask16 = head_mask.astype(BF16)
+
+    def spread(block):
+        return jnp.concatenate([block] * G, axis=0) * head_mask16
+
+    def collect(full):
+        masked = full * head_mask
+        total = masked[:rows]
+        for h in range(1, G):
+            total = total + masked[h * rows : (h + 1) * rows]
+        return total
+
+    settle(got, recv_sem)
+    for s in range(R):
+        for t in range(T):
+            piece = got[s * T + t].astype(F32)
+            rs, cs = slice(s * TILE, (s + 1) * TILE), slice(t * width, (t + 1) * width)
+            x_s[rs, cs] = piece[:TILE]
+            dy_s[rs, cs] = piece[TILE:]
+
+    x = x_s[...]
+    normal, x_scale = norm_parts(x)
+    normed = normal.astype(BF16)
+    wu_copy.wait()
+    wo_copy.wait()
+    projected, slopes_back = [], []
+    for c in range(4):
+        block = mm(normed, wu[:, c * feat : (c + 1) * feat])
+        value, deriv = silu_parts(block)
+        projected.append(value if c == 0 else value.astype(BF16))
+        slopes_back.append(deriv)
+    gate, value, query, key = projected
+
+    relative = slope_s[...]
+    allowed = relative >= 0.0
+    weights, derivs, pieces, values, keys, queries = [], [], [], [], [], []
+    for g in range(H // G):
+        cs = slice(g * gw, (g + 1) * gw)
+        kd, vd, q = spread(key[:, cs]), spread(value[:, cs]), query[:, cs]
+        slope = jnp.zeros((1, gr), F32)
+        for h in range(G):
+            slope = jnp.where(lane // rows == h, slope_ref[g * G + h], slope)
+        scores = mm(q, kd, NT) * scale - slope * relative
+        weight, deriv = silu_parts(scores)
+        weight = jnp.where(allowed, weight, 0.0).astype(BF16)
+        derivs.append(jnp.where(allowed, deriv * scale, 0.0))
+        weights.append(weight)
+        pieces.append(mm(weight, vd))
+        keys.append(kd)
+        values.append(vd)
+        queries.append(q)
+    attended, att_scale = norm_parts(jnp.concatenate(pieces, axis=1))
+    gated = (attended * gate).astype(BF16)
+    output = x + mm(gated, wo[...])
+
+    dy = dy_s[...]
+    dgated = mm(dy.astype(BF16), wo[...], NT).astype(BF16).astype(F32)
+    dgate = dgated * attended
+    datt = norm_back(dgated * gate, attended, att_scale).astype(BF16)
+    dv, dq, dk = [], [], []
+    for g in range(H // G):
+        da = datt[:, g * gw : (g + 1) * gw]
+        dw = mm(da, values[g], NT).astype(BF16).astype(F32)
+        ds = (dw * derivs[g]).astype(BF16)
+        dv.append(collect(mm(weights[g], da, TN)))
+        dq.append(mm(ds, keys[g]))
+        dk.append(collect(mm(ds, queries[g], TN)))
+    dprojected = [dgate] + [
+        jnp.concatenate(parts, axis=1).astype(BF16).astype(F32) for parts in (dv, dq, dk)
+    ]
+    dnormed = jnp.zeros_like(x)
+    for c in range(4):
+        dz = (dprojected[c] * slopes_back[c]).astype(BF16)
+        dnormed = dnormed + mm(dz, wu[:, c * feat : (c + 1) * feat], NT)
+    dnormed = dnormed.astype(BF16).astype(F32)
+    gradient = norm_back(dnormed, normal, x_scale) + dy
+
+    for s in range(R):
+        for t in range(T):
+            rs, cs = slice(s * TILE, (s + 1) * TILE), slice(t * width, (t + 1) * width)
+            back[s * T + t] = jnp.concatenate([output[rs, cs], gradient[rs, cs]], axis=0).astype(BF16)
+    post(back, ret, send_sem2, recv_sem2)
+    settle(ret, recv_sem2)
+    for t in range(T):
+        for j in range(0, R, 2):
+            first = ret[inv[t, j] * T + t].astype(F32)
+            second = ret[inv[t, j + 1] * T + t].astype(F32)
+            at = slice(t * rows + j * TILE, t * rows + (j + 2) * TILE)
+            out_ref[at, :] = jnp.concatenate([first[:TILE], second[:TILE]], axis=0).astype(BF16)
+            grad_ref[at, :] = jnp.concatenate([first[TILE:], second[TILE:]], axis=0).astype(BF16)
+    settle(stage, send_sem)
+    settle(back, send_sem2)
+
+
+def fused_shards(
+    embeds, cotangent, send_plan, work_plan, sequence_tiles, slopes, uvqk_weight, out_weight
+):
+    T, R = lax.axis_size("table"), lax.axis_size("replica")
+    n, rows, width = T * R, R * TILE, embeds.shape[1]
+    feat, H = T * width, slopes.shape[0]
+    G = max(1, min(H, MXU // max(feat // H, rows)))
+    vmem = pl.BlockSpec(memory_space=pltpu.VMEM)
+    smem = pl.BlockSpec(memory_space=pltpu.SMEM)
+    hbm = pl.BlockSpec(memory_space=pl.ANY)
+    message = pltpu.VMEM((n, 2 * TILE, width), BF16)
+    return pl.pallas_call(
+        functools.partial(fused_kernel, T, R, H),
+        out_shape=(
+            jax.ShapeDtypeStruct(embeds.shape, BF16),
+            jax.ShapeDtypeStruct(embeds.shape, BF16),
+        ),
+        in_specs=[smem, smem, smem, smem, vmem, vmem, hbm, hbm],
+        out_specs=(vmem, vmem),
+        scratch_shapes=[
+            pltpu.VMEM(uvqk_weight.shape, BF16),
+            pltpu.VMEM(out_weight.shape, BF16),
+            pltpu.VMEM((n, TILE, width), F32),
+            pltpu.VMEM((n, TILE, width), F32),
+            message,
+            message,
+            pltpu.VMEM((rows, feat), F32),
+            pltpu.VMEM((rows, feat), F32),
+            pltpu.VMEM((rows, G * rows), F32),
+            message,
+            message,
+            pltpu.SMEM((T, R), jnp.int32),
+            pltpu.SemaphoreType.DMA((2,)),
+            pltpu.SemaphoreType.DMA,
+            pltpu.SemaphoreType.DMA,
+            pltpu.SemaphoreType.DMA,
+            pltpu.SemaphoreType.DMA,
+        ],
+        compiler_params=pltpu.CompilerParams(
+            collective_id=0, has_side_effects=True, vmem_limit_bytes=48 << 20
+        ),
+        name="hstu_fused",
+    )(send_plan, work_plan, sequence_tiles, slopes, embeds, cotangent, uvqk_weight, out_weight)
+
+
+def fits_fused(embeds, slopes, T, R):
+    width = embeds.shape[1]
+    heads = slopes.shape[0]
+    row_count = embeds.shape[0] // T
+    head_size = width * T // heads
+    return (
+        width % LANES == 0
+        and R % 2 == 0
+        and row_count == R * TILE
+        and head_size == row_count
+        and heads % max(1, min(heads, MXU // head_size)) == 0
+    )
+
+
+def routed(embeds, cotangent, send_plan, work_plan, sequence_tiles, slopes, *weights):
+    T, R = lax.axis_size("table"), lax.axis_size("replica")
+    body = fused_shards if fits_fused(embeds, slopes, T, R) else shards
+    return body(embeds, cotangent, send_plan, work_plan, sequence_tiles, slopes, *weights)
+
+
 def solution(mesh):
     in_specs = (
         P("replica", "table"),
@@ -136,4 +431,4 @@
         P(),
     )
     out_specs = (P("replica", "table"), P("replica", "table"))
-    return jax.shard_map(shards, mesh=mesh, in_specs=in_specs, out_specs=out_specs, check_vma=False)
+    return jax.shard_map(routed, mesh=mesh, in_specs=in_specs, out_specs=out_specs, check_vma=False)

time: 101 us -> 30.6 us (0.30)
  starting transfers between devices: 31.8 us -> 0 us
  matrix products: 25.3 us -> 0 us
  waiting for transfers between devices: 22.5 us -> 0 us
  Pallas kernels: 0 us -> 21.3 us
  local copies, waits for them, and re-layouts: 14 us -> 8.21 us
  other arithmetic: 5.07 us -> 0 us
    all_to_all x8 -> x0, starting transfers between devices: 31.8 us -> none  [the longest x1 5.31 us: shards(): lax.all_to_all(embeds, 'table', split_axis=0, concat_axis=1, tiled=True)]
    dot_general x52 -> x0, matrix products: 25.3 us -> none  [the longest x24 10.2 us: hstu_layer(): jnp.dot(weights, value_part[:, lower:upper], preferred_element_type=jnp.f...]
    all_to_all x8 -> x0, waiting for transfers between devices: 22.5 us -> none  [the longest x1 4.81 us: shards(): lax.all_to_all(to_home(back_grads), 'table', split_axis=1, concat_axis=0,...]
    pallas_call x0 -> x1, Pallas kernels: none -> 21.3 us  [fused_shards(): pl.pallas_call(functools.partial(fused_kernel, T, R, H), out_shape=(jax.S...]
    gather x8 -> x0, local copies, waits for them, and re-layouts: 6.92 us -> none  [the longest x2 2.36 us: to_sources(): return result.reshape(tile_count, TILE, feature_count)[undo_work]]
    unnamed x36 -> x18, local copies, waits for them, and re-layouts: 1.96 us -> 8.21 us
    scatter x2 -> x0, local copies, waits for them, and re-layouts: 1.75 us -> none  [the longest x1 1.15 us: shards(): undo_send = jnp.zeros((tile_count,), jnp.int32).at[own_send].set(tile_order)]
    reduce_sum x5 -> x0, other arithmetic: 1.64 us -> none  [the longest x2 1.31 us: layer_norm(): centred = features - centre]
  transfers between devices with their start and end apart: 8 -> 0, of which waited for: 7 -> 0; matrix products, arithmetic and copies ran while one was open for 31% -> 0% of each run, Pallas kernels for 0% -> 0%
where the time goes in v1:
time: 30.6 us; the launch traced here: 30.2 us
  Pallas kernels  21.3 us (70%)
  local copies, waits for them, and re-layouts  8.21 us (27%)
  between operations  0.66 us (2%)
    pallas_call x1, Pallas kernels, fused_shards(): pl.pallas_call(functools.partial(fused_kernel, T, R, H), out_shape=(jax.S...  21.3 us
    unnamed x18, local copies, waits for them, and re-layouts  8.21 us

profile of v1, /device:TPU:0, one launch (start us, length us, event | category | flops | bytes accessed | tf_op | source)
XLA Modules:
  0.0 30.2 jit_solution(8109271249284702038)
XLA Ops:
  0.6 0.0 copy-start
  0.6 1.6 %copy-done = bf16[512,2048]{1,0:T(8,128)(2,1)S(1)} copy-done((bf16[512,2048]{1,0:T(8,128)(2,1)S(1)}, bf16[512,2048]{1,0:T(8,128)(2,1)}, u32[]{:S(2)}) %copy-start) | copy-done | bytes 2097176
  2.2 0.0 copy-start.1
  2.2 1.0 %copy-done.1 = bf16[512,512]{1,0:T(8,128)(2,1)S(1)} copy-done((bf16[512,512]{1,0:T(8,128)(2,1)S(1)}, bf16[512,512]{1,0:T(8,128)(2,1)}, u32[]{:S(2)}) %copy-start.1) | copy-done | bytes 524312
  3.3 0.0 copy-start.2
  3.3 0.8 %copy-done.2 = bf16[256,128]{1,0:T(8,128)(2,1)S(1)} copy-done((bf16[256,128]{1,0:T(8,128)(2,1)S(1)}, bf16[256,128]{1,0:T(8,128)(2,1)}, u32[]{:S(2)}) %copy-start.2) | copy-done | bytes 65560
  4.1 0.0 copy-start.3
  4.1 0.8 %copy-done.3 = bf16[256,128]{1,0:T(8,128)(2,1)S(1)} copy-done((bf16[256,128]{1,0:T(8,128)(2,1)S(1)}, bf16[256,128]{1,0:T(8,128)(2,1)}, u32[]{:S(2)}) %copy-start.3) | copy-done | bytes 65560
  4.9 0.0 copy-start.4
  4.9 0.7 %copy-done.4 = s32[1,4,8]{2,1,0:T(4,128)S(1)} copy-done((s32[1,4,8]{2,1,0:T(4,128)S(1)}, s32[1,4,8]{2,1,0:T(4,128)}, u32[]{:S(2)}) %copy-start.4) | copy-done | bytes 152
  5.6 0.0 copy-start.5
  5.6 0.7 %copy-done.5 = s32[1,1,8]{2,1,0:T(1,128)S(1)} copy-done((s32[1,1,8]{2,1,0:T(1,128)S(1)}, s32[1,1,8]{2,1,0:T(1,128)}, u32[]{:S(2)}) %copy-start.5) | copy-done | bytes 56
  6.3 0.0 copy-start.6
  6.3 0.7 %copy-done.6 = s32[1,1,4]{2,1,0:T(1,128)S(1)} copy-done((s32[1,1,4]{2,1,0:T(1,128)S(1)}, s32[1,1,4]{2,1,0:T(1,128)}, u32[]{:S(2)}) %copy-start.6) | copy-done | bytes 40
  6.9 0.0 copy-start.7
  6.9 0.7 %copy-done.7 = f32[8]{0:T(128)S(1)} copy-done((f32[8]{0:T(128)S(1)}, f32[8]{0:T(128)}, u32[]{:S(2)}) %copy-start.7) | copy-done | bytes 56
  7.6 21.3 %hstu_fused.1 = (bf16[256,128]{1,0:T(8,128)(2,1)S(1)}, bf16[256,128]{1,0:T(8,128)(2,1)S(1)}) custom-call(s32[1,4,8]{2,1,0:T(4,128)S(1)} %copy-done.4, s32[1,1,8]{2,1,0:T(1,128)S(1)} %copy-done.5, s32[1,1,4]{2,1,0:T(1,128)S(1)} %copy-done.6, f32[8]{0:T(128)S(1)} %copy-done.7, bf16[256,128]{1,0:T(8,128)(2,1)S(1)} %copy-done.2, bf16[256,128]{1,0:T(8,128)(2,1)S(1)} %copy-done.3, ...), custom_call_target="tpu_custom_call" | custom-call | tf_op jit(solution)/shard_map/hstu_fused/pallas_call | solution.py:368
  29.0 0.6 %copy.12 = bf16[256,128]{1,0:T(8,128)(2,1)} copy(bf16[256,128]{1,0:T(8,128)(2,1)S(1)} %get-tuple-element.4) | data formatting | bytes 131072
  29.6 0.6 %copy.13 = bf16[256,128]{1,0:T(8,128)(2,1)} copy(bf16[256,128]{1,0:T(8,128)(2,1)S(1)} %get-tuple-element.5) | data formatting | bytes 131072
Async XLA Ops:
  0.6 1.6 %copy-start = (bf16[512,2048]{1,0:T(8,128)(2,1)S(1)}, bf16[512,2048]{1,0:T(8,128)(2,1)}, u32[]{:S(2)}) copy-start(bf16[512,2048]{1,0:T(8,128)(2,1)} %wu_hbm.1) | copy-start | bytes 6291460
  2.2 1.0 %copy-start.1 = (bf16[512,512]{1,0:T(8,128)(2,1)S(1)}, bf16[512,512]{1,0:T(8,128)(2,1)}, u32[]{:S(2)}) copy-start(bf16[512,512]{1,0:T(8,128)(2,1)} %wo_hbm.1) | copy-start | bytes 1572868
  3.3 0.8 %copy-start.2 = (bf16[256,128]{1,0:T(8,128)(2,1)S(1)}, bf16[256,128]{1,0:T(8,128)(2,1)}, u32[]{:S(2)}) copy-start(bf16[256,128]{1,0:T(8,128)(2,1)} %emb_ref.1) | copy-start | bytes 196612
  4.1 0.8 %copy-start.3 = (bf16[256,128]{1,0:T(8,128)(2,1)S(1)}, bf16[256,128]{1,0:T(8,128)(2,1)}, u32[]{:S(2)}) copy-start(bf16[256,128]{1,0:T(8,128)(2,1)} %cot_ref.1) | copy-start | bytes 196612
  4.9 0.7 %copy-start.4 = (s32[1,4,8]{2,1,0:T(4,128)S(1)}, s32[1,4,8]{2,1,0:T(4,128)}, u32[]{:S(2)}) copy-start(s32[1,4,8]{2,1,0:T(4,128)} %send_ref.1) | copy-start | bytes 388
  5.6 0.7 %copy-start.5 = (s32[1,1,8]{2,1,0:T(1,128)S(1)}, s32[1,1,8]{2,1,0:T(1,128)}, u32[]{:S(2)}) copy-start(s32[1,1,8]{2,1,0:T(1,128)} %work_ref.1) | copy-start | bytes 100
  6.3 0.7 %copy-start.6 = (s32[1,1,4]{2,1,0:T(1,128)S(1)}, s32[1,1,4]{2,1,0:T(1,128)}, u32[]{:S(2)}) copy-start(s32[1,1,4]{2,1,0:T(1,128)} %seq_ref.1) | copy-start | bytes 52
  6.9 0.7 %copy-start.7 = (f32[8]{0:T(128)S(1)}, f32[8]{0:T(128)}, u32[]{:S(2)}) copy-start(f32[8]{0:T(128)} %slope_ref.1) | copy-start | bytes 100

commit v2 on v1

--- a/solution.py
+++ b/solution.py
@@ -10,6 +10,7 @@
 MESH = pl.DeviceIdType.MESH
 MXU = 256
 LANES = 128
+VMEM_BYTES = 64 << 20
 F32 = jnp.float32
 BF16 = jnp.bfloat16
 
@@ -161,10 +162,11 @@
 
 def fused_kernel(
     T, R, H,
-    send_ref, work_ref, seq_ref, slope_ref, emb_ref, cot_ref, wu_hbm, wo_hbm,
-    out_ref, grad_ref,
-    wu, wo, emb32, cot32, stage, got, x_s, dy_s, slope_s, back, ret, inv,
-    w_sem, send_sem, recv_sem, send_sem2, recv_sem2,
+    send_hbm, work_hbm, seq_hbm, slope_hbm, emb_hbm, cot_hbm, wu_hbm, wo_hbm,
+    ret,
+    send_ref, work_ref, seq_ref, slope_ref, emb_ref, cot_ref,
+    wu, wo, emb32, cot32, stage, got, x_s, dy_s, slope_s, back,
+    in_sem, own_sem, send_sem, recv_sem, send_sem2, recv_sem2,
 ):
     n = T * R
     rows = R * TILE
@@ -178,22 +180,28 @@
     me_r = lax.axis_index("replica")
     me = me_r * T + me_t
 
-    wu_copy = pltpu.make_async_copy(wu_hbm, wu, w_sem.at[0])
-    wo_copy = pltpu.make_async_copy(wo_hbm, wo, w_sem.at[1])
-    wu_copy.start()
-    wo_copy.start()
-
-    def peer(off):
-        other = lax.rem(me + off, n)
-        return other, {"table": lax.rem(other, T), "replica": other // T}
+    sources = (send_hbm, emb_hbm, cot_hbm, work_hbm, seq_hbm, slope_hbm, wu_hbm, wo_hbm)
+    targets = (send_ref, emb_ref, cot_ref, work_ref, seq_ref, slope_ref, wu, wo)
+    loads = [
+        pltpu.make_async_copy(source, target, in_sem.at[i])
+        for i, (source, target) in enumerate(zip(sources, targets))
+    ]
+    for load in loads:
+        load.start()
+
+    peers = []
+    for far in range(R - 1, -1, -1):
+        for near in range(T):
+            if far or near:
+                t, r = lax.rem(me_t + near, T), lax.rem(me_r + far, R)
+                peers.append((r * T + t, {"table": t, "replica": r}))
 
     barrier = pltpu.get_barrier_semaphore()
-
-    def greet(off, carry):
-        pl.semaphore_signal(barrier, inc=1, device_id=peer(off)[1], device_id_type=MESH)
-        return carry
-
-    lax.fori_loop(1, n, greet, 0)
+    for _, device in peers:
+        pl.semaphore_signal(barrier, inc=1, device_id=device, device_id_type=MESH)
+
+    for load in loads[:3]:
+        load.wait()
 
     emb32[...] = emb_ref[...].astype(F32).reshape(emb32.shape)
     cot32[...] = cot_ref[...].astype(F32).reshape(cot32.shape)
@@ -205,8 +213,7 @@
     pl.semaphore_wait(barrier, n - 1)
 
     def post(src, dst, s_sem, r_sem):
-        def one(off, carry):
-            other, device = peer(off)
+        for other, device in peers:
             pltpu.make_async_remote_copy(
                 src_ref=src.at[other],
                 dst_ref=dst.at[me],
@@ -215,24 +222,16 @@
                 device_id=device,
                 device_id_type=MESH,
             ).start()
-            return carry
-
-        lax.fori_loop(1, n, one, 0)
-        dst[me] = src[me]
 
     def settle(ref, sem):
         part = ref.at[pl.ds(0, n - 1)]
         pltpu.make_async_copy(part, part, sem).wait()
 
     post(stage, got, send_sem, recv_sem)
-
-    for t in range(T):
-        for j in range(R):
-            found = jnp.int32(0)
-            for d in range(1, R):
-                found = jnp.where(send_ref[0, t, d] == j, d, found)
-            inv[t, j] = found
-
+    got[me] = stage[me]
+
+    for load in loads[3:6]:
+        load.wait()
     bounds = []
     total = jnp.int32(0)
     for j in range(seq_ref.shape[2]):
@@ -283,8 +282,8 @@
     x = x_s[...]
     normal, x_scale = norm_parts(x)
     normed = normal.astype(BF16)
-    wu_copy.wait()
-    wo_copy.wait()
+    for load in loads[6:]:
+        load.wait()
     projected, slopes_back = [], []
     for c in range(4):
         block = mm(normed, wu[:, c * feat : (c + 1) * feat])
@@ -342,14 +341,10 @@
             rs, cs = slice(s * TILE, (s + 1) * TILE), slice(t * width, (t + 1) * width)
             back[s * T + t] = jnp.concatenate([output[rs, cs], gradient[rs, cs]], axis=0).astype(BF16)
     post(back, ret, send_sem2, recv_sem2)
+    own = pltpu.make_async_copy(back.at[me], ret.at[me], own_sem)
+    own.start()
+    own.wait()
     settle(ret, recv_sem2)
-    for t in range(T):
-        for j in range(0, R, 2):
-            first = ret[inv[t, j] * T + t].astype(F32)
-            second = ret[inv[t, j + 1] * T + t].astype(F32)
-            at = slice(t * rows + j * TILE, t * rows + (j + 2) * TILE)
-            out_ref[at, :] = jnp.concatenate([first[:TILE], second[:TILE]], axis=0).astype(BF16)
-            grad_ref[at, :] = jnp.concatenate([first[TILE:], second[TILE:]], axis=0).astype(BF16)
     settle(stage, send_sem)
     settle(back, send_sem2)
 
@@ -363,17 +358,20 @@
     G = max(1, min(H, MXU // max(feat // H, rows)))
     vmem = pl.BlockSpec(memory_space=pltpu.VMEM)
     smem = pl.BlockSpec(memory_space=pltpu.SMEM)
-    hbm = pl.BlockSpec(memory_space=pl.ANY)
+    hbm = pl.BlockSpec(memory_space=pltpu.HBM)
     message = pltpu.VMEM((n, 2 * TILE, width), BF16)
-    return pl.pallas_call(
+    ret = pl.pallas_call(
         functools.partial(fused_kernel, T, R, H),
-        out_shape=(
-            jax.ShapeDtypeStruct(embeds.shape, BF16),
-            jax.ShapeDtypeStruct(embeds.shape, BF16),
-        ),
-        in_specs=[smem, smem, smem, smem, vmem, vmem, hbm, hbm],
-        out_specs=(vmem, vmem),
+        out_shape=jax.ShapeDtypeStruct((n, 2 * TILE, width), BF16),
+        in_specs=[hbm] * 8,
+        out_specs=hbm,
         scratch_shapes=[
+            pltpu.SMEM(send_plan.shape, jnp.int32),
+            pltpu.SMEM(work_plan.shape, jnp.int32),
+            pltpu.SMEM(sequence_tiles.shape, jnp.int32),
+            pltpu.SMEM(slopes.shape, F32),
+            pltpu.VMEM(embeds.shape, BF16),
+            pltpu.VMEM(cotangent.shape, BF16),
             pltpu.VMEM(uvqk_weight.shape, BF16),
             pltpu.VMEM(out_weight.shape, BF16),
             pltpu.VMEM((n, TILE, width), F32),
@@ -384,19 +382,44 @@
             pltpu.VMEM((rows, feat), F32),
             pltpu.VMEM((rows, G * rows), F32),
             message,
-            message,
-            pltpu.SMEM((T, R), jnp.int32),
-            pltpu.SemaphoreType.DMA((2,)),
+            pltpu.SemaphoreType.DMA((8,)),
+            pltpu.SemaphoreType.DMA,
             pltpu.SemaphoreType.DMA,
             pltpu.SemaphoreType.DMA,
             pltpu.SemaphoreType.DMA,
             pltpu.SemaphoreType.DMA,
         ],
         compiler_params=pltpu.CompilerParams(
-            collective_id=0, has_side_effects=True, vmem_limit_bytes=48 << 20
+            collective_id=0, has_side_effects=True, vmem_limit_bytes=VMEM_BYTES
         ),
         name="hstu_fused",
     )(send_plan, work_plan, sequence_tiles, slopes, embeds, cotangent, uvqk_weight, out_weight)
+    return pl.pallas_call(
+        functools.partial(place_kernel, T, R),
+        out_shape=(
+            jax.ShapeDtypeStruct(embeds.shape, BF16),
+            jax.ShapeDtypeStruct(embeds.shape, BF16),
+        ),
+        in_specs=[smem, vmem],
+        out_specs=(vmem, vmem),
+        scratch_shapes=[
+            pltpu.VMEM((n, TILE, width), F32),
+            pltpu.VMEM((n, TILE, width), F32),
+        ],
+        compiler_params=pltpu.CompilerParams(vmem_limit_bytes=VMEM_BYTES),
+        name="place",
+    )(send_plan, ret)
+
+
+def place_kernel(T, R, send_ref, ret_ref, out_ref, grad_ref, out32, grad32):
+    for t in range(T):
+        for d in range(R):
+            piece = ret_ref[d * T + t].astype(F32)
+            k = t * R + send_ref[0, t, d]
+            out32[k] = piece[:TILE]
+            grad32[k] = piece[TILE:]
+    out_ref[...] = out32[...].reshape(out_ref.shape).astype(BF16)
+    grad_ref[...] = grad32[...].reshape(grad_ref.shape).astype(BF16)
 
 
 def fits_fused(embeds, slopes, T, R):

time: 30.6 us -> 23.7 us (0.77)
  local copies, waits for them, and re-layouts: 8.21 us -> 0 us
  Pallas kernels: 21.3 us -> 22.8 us
    unnamed x18 -> x0, local copies, waits for them, and re-layouts: 8.21 us -> none
    pallas_call x1 -> x2, Pallas kernels: 21.3 us -> 22.8 us  [the longest x1 21.2 us: fused_shards(): pl.pallas_call(functools.partial(fused_kernel, T, R, H), out_shape=jax.Sh...]
where the time goes in v2:
time: 23.7 us; the launch traced here: 23.5 us
  Pallas kernels  22.8 us (96%)
  between operations  0.64 us (3%)
    pallas_call x1, Pallas kernels, fused_shards(): pl.pallas_call(functools.partial(fused_kernel, T, R, H), out_shape=jax.Sh...  21.2 us
    pallas_call x1, Pallas kernels, fused_shards(): pl.pallas_call(functools.partial(place_kernel, T, R), out_shape=(jax.Shap...  1.61 us

profile of v2, /device:TPU:0, one launch (start us, length us, event | category | flops | bytes accessed | tf_op | source)
XLA Modules:
  0.0 23.5 jit_solution(15879424345499472956)
XLA Ops:
  0.6 21.2 %hstu_fused.1.ret_ref = bf16[32,16,128]{2,1,0:T(8,128)(2,1)} custom-call(s32[1,4,8]{2,1,0:T(4,128)} %send_ref.1, s32[1,1,8]{2,1,0:T(1,128)} %work_hbm.1, s32[1,1,4]{2,1,0:T(1,128)} %seq_hbm.1, f32[8]{0:T(128)} %slope_hbm.1, bf16[256,128]{1,0:T(8,128)(2,1)} %emb_hbm.1, bf16[256,128]{1,0:T(8,128)(2,1)} %cot_hbm.1, bf16[512,2048]{1,0:T(8,128)(2,1)} %wu_hbm.1, ...), custom_call_target="tpu_custom_call" | custom-call | tf_op jit(solution)/shard_map/hstu_fused/pallas_call | solution.py:363
  21.8 1.6 %place.1 = (bf16[256,128]{1,0:T(8,128)(2,1)}, bf16[256,128]{1,0:T(8,128)(2,1)}) custom-call(s32[1,4,8]{2,1,0:T(4,128)} %send_ref.1, bf16[32,16,128]{2,1,0:T(8,128)(2,1)} %hstu_fused.1.ret_ref), custom_call_target="tpu_custom_call" | custom-call | tf_op jit(solution)/shard_map/place/pallas_call | solution.py:397

commit v3 on v2

--- a/solution.py
+++ b/solution.py
@@ -163,10 +163,11 @@
 def fused_kernel(
     T, R, H,
     send_hbm, work_hbm, seq_hbm, slope_hbm, emb_hbm, cot_hbm, wu_hbm, wo_hbm,
-    ret,
+    out_ret, grad_ret,
     send_ref, work_ref, seq_ref, slope_ref, emb_ref, cot_ref,
-    wu, wo, emb32, cot32, stage, got, x_s, dy_s, slope_s, back,
-    in_sem, own_sem, send_sem, recv_sem, send_sem2, recv_sem2,
+    wu, wo, emb32, cot32, emb_stage, cot_stage, emb_got, cot_got, x_s, dy_s, slope_s,
+    out_back, grad_back,
+    in_sem, own_sem, send_sem, recv_sem,
 ):
     n = T * R
     rows = R * TILE
@@ -186,7 +187,7 @@
         pltpu.make_async_copy(source, target, in_sem.at[i])
         for i, (source, target) in enumerate(zip(sources, targets))
     ]
-    for load in loads:
+    for load in loads[:6]:
         load.start()
 
     peers = []
@@ -200,25 +201,24 @@
     for _, device in peers:
         pl.semaphore_signal(barrier, inc=1, device_id=device, device_id_type=MESH)
 
-    for load in loads[:3]:
-        load.wait()
-
-    emb32[...] = emb_ref[...].astype(F32).reshape(emb32.shape)
-    cot32[...] = cot_ref[...].astype(F32).reshape(cot32.shape)
-    for d in range(R):
-        for t in range(T):
-            k = t * R + send_ref[0, t, d]
-            stage[d * T + t] = jnp.concatenate([emb32[k], cot32[k]], axis=0).astype(BF16)
-
+    def gather(source, source32, target):
+        source32[...] = source[...].astype(F32).reshape(source32.shape)
+        for d in range(R):
+            for t in range(T):
+                target[d * T + t] = source32[t * R + send_ref[0, t, d]].astype(BF16)
+
+    loads[0].wait()
+    loads[1].wait()
+    gather(emb_ref, emb32, emb_stage)
     pl.semaphore_wait(barrier, n - 1)
 
-    def post(src, dst, s_sem, r_sem):
+    def post(src, dst, index):
         for other, device in peers:
             pltpu.make_async_remote_copy(
                 src_ref=src.at[other],
                 dst_ref=dst.at[me],
-                send_sem=s_sem,
-                recv_sem=r_sem,
+                send_sem=send_sem.at[index],
+                recv_sem=recv_sem.at[index],
                 device_id=device,
                 device_id_type=MESH,
             ).start()
@@ -227,8 +227,28 @@
         part = ref.at[pl.ds(0, n - 1)]
         pltpu.make_async_copy(part, part, sem).wait()
 
-    post(stage, got, send_sem, recv_sem)
-    got[me] = stage[me]
+    def scatter(source, target):
+        for s in range(R):
+            for t in range(T):
+                target[s * T + t] = source[
+                    s * TILE : (s + 1) * TILE, t * width : (t + 1) * width
+                ].astype(BF16)
+
+    def unpack(source, target):
+        for s in range(R):
+            for t in range(T):
+                target[s * TILE : (s + 1) * TILE, t * width : (t + 1) * width] = source[
+                    s * T + t
+                ].astype(F32)
+
+    post(emb_stage, emb_got, 0)
+    emb_got[me] = emb_stage[me]
+    loads[2].wait()
+    gather(cot_ref, cot32, cot_stage)
+    post(cot_stage, cot_got, 1)
+    cot_got[me] = cot_stage[me]
+    for load in loads[6:]:
+        load.start()
 
     for load in loads[3:6]:
         load.wait()
@@ -271,14 +291,8 @@
             total = total + masked[h * rows : (h + 1) * rows]
         return total
 
-    settle(got, recv_sem)
-    for s in range(R):
-        for t in range(T):
-            piece = got[s * T + t].astype(F32)
-            rs, cs = slice(s * TILE, (s + 1) * TILE), slice(t * width, (t + 1) * width)
-            x_s[rs, cs] = piece[:TILE]
-            dy_s[rs, cs] = piece[TILE:]
-
+    settle(emb_got, recv_sem.at[0])
+    unpack(emb_got, x_s)
     x = x_s[...]
     normal, x_scale = norm_parts(x)
     normed = normal.astype(BF16)
@@ -314,6 +328,13 @@
     gated = (attended * gate).astype(BF16)
     output = x + mm(gated, wo[...])
 
+    scatter(output, out_back)
+    post(out_back, out_ret, 2)
+    out_own = pltpu.make_async_copy(out_back.at[me], out_ret.at[me], own_sem.at[0])
+    out_own.start()
+
+    settle(cot_got, recv_sem.at[1])
+    unpack(cot_got, dy_s)
     dy = dy_s[...]
     dgated = mm(dy.astype(BF16), wo[...], NT).astype(BF16).astype(F32)
     dgate = dgated * attended
@@ -336,17 +357,16 @@
     dnormed = dnormed.astype(BF16).astype(F32)
     gradient = norm_back(dnormed, normal, x_scale) + dy
 
-    for s in range(R):
-        for t in range(T):
-            rs, cs = slice(s * TILE, (s + 1) * TILE), slice(t * width, (t + 1) * width)
-            back[s * T + t] = jnp.concatenate([output[rs, cs], gradient[rs, cs]], axis=0).astype(BF16)
-    post(back, ret, send_sem2, recv_sem2)
-    own = pltpu.make_async_copy(back.at[me], ret.at[me], own_sem)
-    own.start()
-    own.wait()
-    settle(ret, recv_sem2)
-    settle(stage, send_sem)
-    settle(back, send_sem2)
+    scatter(gradient, grad_back)
+    post(grad_back, grad_ret, 3)
+    grad_own = pltpu.make_async_copy(grad_back.at[me], grad_ret.at[me], own_sem.at[1])
+    grad_own.start()
+    out_own.wait()
+    grad_own.wait()
+    for index, source in enumerate((emb_stage, cot_stage, out_back, grad_back)):
+        settle(source, send_sem.at[index])
+    settle(out_ret, recv_sem.at[2])
+    settle(grad_ret, recv_sem.at[3])
 
 
 def fused_shards(
@@ -356,15 +376,15 @@
     n, rows, width = T * R, R * TILE, embeds.shape[1]
     feat, H = T * width, slopes.shape[0]
     G = max(1, min(H, MXU // max(feat // H, rows)))
-    vmem = pl.BlockSpec(memory_space=pltpu.VMEM)
     smem = pl.BlockSpec(memory_space=pltpu.SMEM)
     hbm = pl.BlockSpec(memory_space=pltpu.HBM)
-    message = pltpu.VMEM((n, 2 * TILE, width), BF16)
-    ret = pl.pallas_call(
+    message = pltpu.VMEM((n, TILE, width), BF16)
+    tiles = jax.ShapeDtypeStruct((n, TILE, width), BF16)
+    results = pl.pallas_call(
         functools.partial(fused_kernel, T, R, H),
-        out_shape=jax.ShapeDtypeStruct((n, 2 * TILE, width), BF16),
+        out_shape=(tiles, tiles),
         in_specs=[hbm] * 8,
-        out_specs=hbm,
+        out_specs=(hbm, hbm),
         scratch_shapes=[
             pltpu.SMEM(send_plan.shape, jnp.int32),
             pltpu.SMEM(work_plan.shape, jnp.int32),
@@ -378,48 +398,44 @@
             pltpu.VMEM((n, TILE, width), F32),
             message,
             message,
+            message,
+            message,
             pltpu.VMEM((rows, feat), F32),
             pltpu.VMEM((rows, feat), F32),
             pltpu.VMEM((rows, G * rows), F32),
             message,
+            message,
             pltpu.SemaphoreType.DMA((8,)),
-            pltpu.SemaphoreType.DMA,
-            pltpu.SemaphoreType.DMA,
-            pltpu.SemaphoreType.DMA,
-            pltpu.SemaphoreType.DMA,
-            pltpu.SemaphoreType.DMA,
+            pltpu.SemaphoreType.DMA((2,)),
+            pltpu.SemaphoreType.DMA((4,)),
+            pltpu.SemaphoreType.DMA((4,)),
         ],
         compiler_params=pltpu.CompilerParams(
             collective_id=0, has_side_effects=True, vmem_limit_bytes=VMEM_BYTES
         ),
         name="hstu_fused",
     )(send_plan, work_plan, sequence_tiles, slopes, embeds, cotangent, uvqk_weight, out_weight)
-    return pl.pallas_call(
+    placed = pl.pallas_call(
         functools.partial(place_kernel, T, R),
-        out_shape=(
-            jax.ShapeDtypeStruct(embeds.shape, BF16),
-            jax.ShapeDtypeStruct(embeds.shape, BF16),
-        ),
-        in_specs=[smem, vmem],
-        out_specs=(vmem, vmem),
-        scratch_shapes=[
-            pltpu.VMEM((n, TILE, width), F32),
-            pltpu.VMEM((n, TILE, width), F32),
-        ],
+        out_shape=(tiles, tiles),
+        in_specs=[smem, hbm, hbm],
+        out_specs=(hbm, hbm),
+        scratch_shapes=[pltpu.SemaphoreType.DMA((2,))],
         compiler_params=pltpu.CompilerParams(vmem_limit_bytes=VMEM_BYTES),
         name="place",
-    )(send_plan, ret)
-
-
-def place_kernel(T, R, send_ref, ret_ref, out_ref, grad_ref, out32, grad32):
+    )(send_plan, *results)
+    return tuple(part.reshape(embeds.shape) for part in placed)
+
+
+def place_kernel(T, R, send_ref, out_ret, grad_ret, out_home, grad_home, sem):
     for t in range(T):
         for d in range(R):
-            piece = ret_ref[d * T + t].astype(F32)
-            k = t * R + send_ref[0, t, d]
-            out32[k] = piece[:TILE]
-            grad32[k] = piece[TILE:]
-    out_ref[...] = out32[...].reshape(out_ref.shape).astype(BF16)
-    grad_ref[...] = grad32[...].reshape(grad_ref.shape).astype(BF16)
+            home = t * R + send_ref[0, t, d]
+            slot = d * T + t
+            pltpu.make_async_copy(out_ret.at[slot], out_home.at[home], sem.at[0]).start()
+            pltpu.make_async_copy(grad_ret.at[slot], grad_home.at[home], sem.at[1]).start()
+    pltpu.make_async_copy(out_home, out_home, sem.at[0]).wait()
+    pltpu.make_async_copy(grad_home, grad_home, sem.at[1]).wait()
 
 
 def fits_fused(embeds, slopes, T, R):

time: 23.7 us -> 27 us (1.14)
  Pallas kernels: 22.8 us -> 26.2 us
    pallas_call x2, Pallas kernels: 22.8 us -> 26.2 us  [the longest x1 20.4 us: fused_shards(): pl.pallas_call(functools.partial(fused_kernel, T, R, H), out_shape=(tiles...]
where the time goes in v3:
time: 27 us; the launch traced here: 26.8 us
  Pallas kernels  26.2 us (97%)
  between operations  0.64 us (2%)
    pallas_call x1, Pallas kernels, fused_shards(): pl.pallas_call(functools.partial(fused_kernel, T, R, H), out_shape=(tiles...  20.4 us
    pallas_call x1, Pallas kernels, fused_shards(): pl.pallas_call(functools.partial(place_kernel, T, R), out_shape=(tiles, t...  5.79 us

profile of v3, /device:TPU:0, one launch (start us, length us, event | category | flops | bytes accessed | tf_op | source)
XLA Modules:
  0.0 26.8 jit_solution(3239846209712971268)
XLA Ops:
  0.6 20.4 %hstu_fused.1 = (bf16[32,8,128]{2,1,0:T(8,128)(2,1)}, bf16[32,8,128]{2,1,0:T(8,128)(2,1)}) custom-call(s32[1,4,8]{2,1,0:T(4,128)} %send_ref.1, s32[1,1,8]{2,1,0:T(1,128)} %work_hbm.1, s32[1,1,4]{2,1,0:T(1,128)} %seq_hbm.1, f32[8]{0:T(128)} %slope_hbm.1, bf16[256,128]{1,0:T(8,128)(2,1)} %emb_hbm.1, bf16[256,128]{1,0:T(8,128)(2,1)} %cot_hbm.1, ...), custom_call_target="tpu_custom_call" | custom-call | tf_op jit(solution)/shard_map/hstu_fused/pallas_call | solution.py:383
  21.0 5.8 %place.1 = (bf16[32,8,128]{2,1,0:T(8,128)(2,1)}, bf16[32,8,128]{2,1,0:T(8,128)(2,1)}) custom-call(s32[1,4,8]{2,1,0:T(4,128)} %send_ref.1, bf16[32,8,128]{2,1,0:T(8,128)(2,1)} %get-tuple-element.6.out_ret, bf16[32,8,128]{2,1,0:T(8,128)(2,1)} %get-tuple-element.7.grad_ret), custom_call_target="tpu_custom_call" | custom-call | tf_op jit(solution)/shard_map/place/pallas_call | solution.py:418

commit v4 on v3

--- a/solution.py
+++ b/solution.py
@@ -420,22 +420,35 @@
         out_shape=(tiles, tiles),
         in_specs=[smem, hbm, hbm],
         out_specs=(hbm, hbm),
-        scratch_shapes=[pltpu.SemaphoreType.DMA((2,))],
+        scratch_shapes=[message] * 4 + [pltpu.SemaphoreType.DMA((4,))],
         compiler_params=pltpu.CompilerParams(vmem_limit_bytes=VMEM_BYTES),
         name="place",
     )(send_plan, *results)
     return tuple(part.reshape(embeds.shape) for part in placed)
 
 
-def place_kernel(T, R, send_ref, out_ret, grad_ret, out_home, grad_home, sem):
-    for t in range(T):
+def place_kernel(
+    T, R, send_ref, out_ret, grad_ret, out_home, grad_home, out_got, grad_got, out_put, grad_put, sem
+):
+    loads = [
+        pltpu.make_async_copy(out_ret, out_got, sem.at[0]),
+        pltpu.make_async_copy(grad_ret, grad_got, sem.at[1]),
+    ]
+    stores = [
+        pltpu.make_async_copy(out_put, out_home, sem.at[2]),
+        pltpu.make_async_copy(grad_put, grad_home, sem.at[3]),
+    ]
+    for load in loads:
+        load.start()
+    homes = [[t * R + send_ref[0, t, d] for t in range(T)] for d in range(R)]
+    for load, store, got, put in zip(loads, stores, (out_got, grad_got), (out_put, grad_put)):
+        load.wait()
         for d in range(R):
-            home = t * R + send_ref[0, t, d]
-            slot = d * T + t
-            pltpu.make_async_copy(out_ret.at[slot], out_home.at[home], sem.at[0]).start()
-            pltpu.make_async_copy(grad_ret.at[slot], grad_home.at[home], sem.at[1]).start()
-    pltpu.make_async_copy(out_home, out_home, sem.at[0]).wait()
-    pltpu.make_async_copy(grad_home, grad_home, sem.at[1]).wait()
+            for t in range(T):
+                put[homes[d][t]] = got[d * T + t]
+        store.start()
+    for store in stores:
+        store.wait()
 
 
 def fits_fused(embeds, slopes, T, R):

time: 27 us -> 23.5 us (0.87)
  Pallas kernels: 26.2 us -> 22.6 us
    pallas_call x1, Pallas kernels: 5.79 us -> 2.25 us  [fused_shards(): pl.pallas_call(functools.partial(place_kernel, T, R), out_shape=(tiles, t...]
where the time goes in v4:
time: 23.5 us; the launch traced here: 23.3 us
  Pallas kernels  22.6 us (96%)
  between operations  0.64 us (3%)
    pallas_call x1, Pallas kernels, fused_shards(): pl.pallas_call(functools.partial(fused_kernel, T, R, H), out_shape=(tiles...  20.4 us
    pallas_call x1, Pallas kernels, fused_shards(): pl.pallas_call(functools.partial(place_kernel, T, R), out_shape=(tiles, t...  2.25 us

profile of v4, /device:TPU:0, one launch (start us, length us, event | category | flops | bytes accessed | tf_op | source)
XLA Modules:
  0.0 23.3 jit_solution(11897110740913022470)
XLA Ops:
  0.6 20.4 %hstu_fused.1 = (bf16[32,8,128]{2,1,0:T(8,128)(2,1)}, bf16[32,8,128]{2,1,0:T(8,128)(2,1)}) custom-call(s32[1,4,8]{2,1,0:T(4,128)} %send_ref.1, s32[1,1,8]{2,1,0:T(1,128)} %work_hbm.1, s32[1,1,4]{2,1,0:T(1,128)} %seq_hbm.1, f32[8]{0:T(128)} %slope_hbm.1, bf16[256,128]{1,0:T(8,128)(2,1)} %emb_hbm.1, bf16[256,128]{1,0:T(8,128)(2,1)} %cot_hbm.1, ...), custom_call_target="tpu_custom_call" | custom-call | tf_op jit(solution)/shard_map/hstu_fused/pallas_call | solution.py:383
  21.0 2.2 %place.1 = (bf16[32,8,128]{2,1,0:T(8,128)(2,1)}, bf16[32,8,128]{2,1,0:T(8,128)(2,1)}) custom-call(s32[1,4,8]{2,1,0:T(4,128)} %send_ref.1, bf16[32,8,128]{2,1,0:T(8,128)(2,1)} %get-tuple-element.6.out_ret, bf16[32,8,128]{2,1,0:T(8,128)(2,1)} %get-tuple-element.7.grad_ret), custom_call_target="tpu_custom_call" | custom-call | tf_op jit(solution)/shard_map/place/pallas_call | solution.py:418

commit v5 on v3

--- a/solution.py
+++ b/solution.py
@@ -163,15 +163,15 @@
 def fused_kernel(
     T, R, H,
     send_hbm, work_hbm, seq_hbm, slope_hbm, emb_hbm, cot_hbm, wu_hbm, wo_hbm,
-    out_ret, grad_ret,
+    ret,
     send_ref, work_ref, seq_ref, slope_ref, emb_ref, cot_ref,
-    wu, wo, emb32, cot32, emb_stage, cot_stage, emb_got, cot_got, x_s, dy_s, slope_s,
+    wu, wo, emb_stage, cot_stage, emb_got, cot_got, x_s, dy_s, slope_s,
     out_back, grad_back,
     in_sem, own_sem, send_sem, recv_sem,
 ):
     n = T * R
     rows = R * TILE
-    width = emb_ref.shape[1]
+    width = emb_ref.shape[2]
     feat = T * width
     hs = feat // H
     G = max(1, min(H, MXU // max(hs, rows)))
@@ -190,33 +190,40 @@
     for load in loads[:6]:
         load.start()
 
+    def partner(own, step, count):
+        other, bit = jnp.int32(0), 1
+        while bit < count:
+            held = lax.rem(lax.div(own, bit), 2)
+            other = other + bit * (1 - held if step & bit else held)
+            bit = 2 * bit
+        return other
+
     peers = []
     for far in range(R - 1, -1, -1):
-        for near in range(T):
+        for near in range(T - 1, -1, -1):
             if far or near:
-                t, r = lax.rem(me_t + near, T), lax.rem(me_r + far, R)
+                t, r = partner(me_t, near, T), partner(me_r, far, R)
                 peers.append((r * T + t, {"table": t, "replica": r}))
 
     barrier = pltpu.get_barrier_semaphore()
     for _, device in peers:
         pl.semaphore_signal(barrier, inc=1, device_id=device, device_id_type=MESH)
 
-    def gather(source, source32, target):
-        source32[...] = source[...].astype(F32).reshape(source32.shape)
+    def gather(source, target):
         for d in range(R):
             for t in range(T):
-                target[d * T + t] = source32[t * R + send_ref[0, t, d]].astype(BF16)
+                target[d * T + t] = source[t * R + send_ref[0, t, d]]
 
     loads[0].wait()
     loads[1].wait()
-    gather(emb_ref, emb32, emb_stage)
+    gather(emb_ref, emb_stage)
     pl.semaphore_wait(barrier, n - 1)
 
-    def post(src, dst, index):
+    def post(src, dst, index, base=0):
         for other, device in peers:
             pltpu.make_async_remote_copy(
                 src_ref=src.at[other],
-                dst_ref=dst.at[me],
+                dst_ref=dst.at[base + me],
                 send_sem=send_sem.at[index],
                 recv_sem=recv_sem.at[index],
                 device_id=device,
@@ -244,7 +251,7 @@
     post(emb_stage, emb_got, 0)
     emb_got[me] = emb_stage[me]
     loads[2].wait()
-    gather(cot_ref, cot32, cot_stage)
+    gather(cot_ref, cot_stage)
     post(cot_stage, cot_got, 1)
     cot_got[me] = cot_stage[me]
     for load in loads[6:]:
@@ -329,8 +336,8 @@
     output = x + mm(gated, wo[...])
 
     scatter(output, out_back)
-    post(out_back, out_ret, 2)
-    out_own = pltpu.make_async_copy(out_back.at[me], out_ret.at[me], own_sem.at[0])
+    post(out_back, ret, 2)
+    out_own = pltpu.make_async_copy(out_back.at[me], ret.at[me], own_sem.at[0])
     out_own.start()
 
     settle(cot_got, recv_sem.at[1])
@@ -358,15 +365,15 @@
     gradient = norm_back(dnormed, normal, x_scale) + dy
 
     scatter(gradient, grad_back)
-    post(grad_back, grad_ret, 3)
-    grad_own = pltpu.make_async_copy(grad_back.at[me], grad_ret.at[me], own_sem.at[1])
+    post(grad_back, ret, 3, n)
+    grad_own = pltpu.make_async_copy(grad_back.at[me], ret.at[n + me], own_sem.at[1])
     grad_own.start()
     out_own.wait()
     grad_own.wait()
     for index, source in enumerate((emb_stage, cot_stage, out_back, grad_back)):
         settle(source, send_sem.at[index])
-    settle(out_ret, recv_sem.at[2])
-    settle(grad_ret, recv_sem.at[3])
+    settle(out_back, recv_sem.at[2])
+    settle(grad_back, recv_sem.at[3])
 
 
 def fused_shards(
@@ -376,26 +383,25 @@
     n, rows, width = T * R, R * TILE, embeds.shape[1]
     feat, H = T * width, slopes.shape[0]
     G = max(1, min(H, MXU // max(feat // H, rows)))
+    vmem = pl.BlockSpec(memory_space=pltpu.VMEM)
     smem = pl.BlockSpec(memory_space=pltpu.SMEM)
     hbm = pl.BlockSpec(memory_space=pltpu.HBM)
     message = pltpu.VMEM((n, TILE, width), BF16)
     tiles = jax.ShapeDtypeStruct((n, TILE, width), BF16)
-    results = pl.pallas_call(
+    ret = pl.pallas_call(
         functools.partial(fused_kernel, T, R, H),
-        out_shape=(tiles, tiles),
+        out_shape=jax.ShapeDtypeStruct((2 * n, TILE, width), BF16),
         in_specs=[hbm] * 8,
-        out_specs=(hbm, hbm),
+        out_specs=hbm,
         scratch_shapes=[
             pltpu.SMEM(send_plan.shape, jnp.int32),
             pltpu.SMEM(work_plan.shape, jnp.int32),
             pltpu.SMEM(sequence_tiles.shape, jnp.int32),
             pltpu.SMEM(slopes.shape, F32),
-            pltpu.VMEM(embeds.shape, BF16),
-            pltpu.VMEM(cotangent.shape, BF16),
+            message,
+            message,
             pltpu.VMEM(uvqk_weight.shape, BF16),
             pltpu.VMEM(out_weight.shape, BF16),
-            pltpu.VMEM((n, TILE, width), F32),
-            pltpu.VMEM((n, TILE, width), F32),
             message,
             message,
             message,
@@ -414,28 +420,33 @@
             collective_id=0, has_side_effects=True, vmem_limit_bytes=VMEM_BYTES
         ),
         name="hstu_fused",
-    )(send_plan, work_plan, sequence_tiles, slopes, embeds, cotangent, uvqk_weight, out_weight)
+    )(
+        send_plan,
+        work_plan,
+        sequence_tiles,
+        slopes,
+        embeds.reshape(tiles.shape),
+        cotangent.reshape(tiles.shape),
+        uvqk_weight,
+        out_weight,
+    )
     placed = pl.pallas_call(
         functools.partial(place_kernel, T, R),
         out_shape=(tiles, tiles),
-        in_specs=[smem, hbm, hbm],
-        out_specs=(hbm, hbm),
-        scratch_shapes=[pltpu.SemaphoreType.DMA((2,))],
+        in_specs=[smem, vmem],
+        out_specs=(vmem, vmem),
         compiler_params=pltpu.CompilerParams(vmem_limit_bytes=VMEM_BYTES),
         name="place",
-    )(send_plan, *results)
+    )(send_plan, ret)
     return tuple(part.reshape(embeds.shape) for part in placed)
 
 
-def place_kernel(T, R, send_ref, out_ret, grad_ret, out_home, grad_home, sem):
+def place_kernel(T, R, send_ref, ret_ref, out_ref, grad_ref):
     for t in range(T):
         for d in range(R):
             home = t * R + send_ref[0, t, d]
-            slot = d * T + t
-            pltpu.make_async_copy(out_ret.at[slot], out_home.at[home], sem.at[0]).start()
-            pltpu.make_async_copy(grad_ret.at[slot], grad_home.at[home], sem.at[1]).start()
-    pltpu.make_async_copy(out_home, out_home, sem.at[0]).wait()
-    pltpu.make_async_copy(grad_home, grad_home, sem.at[1]).wait()
+            out_ref[home] = ret_ref[d * T + t]
+            grad_ref[home] = ret_ref[T * R + d * T + t]
 
 
 def fits_fused(embeds, slopes, T, R):
@@ -445,7 +456,8 @@
     head_size = width * T // heads
     return (
         width % LANES == 0
-        and R % 2 == 0
+        and R & (R - 1) == 0
+        and T & (T - 1) == 0
         and row_count == R * TILE
         and head_size == row_count
         and heads % max(1, min(heads, MXU // head_size)) == 0

time: 27 us -> 22.2 us (0.82)
  Pallas kernels: 26.2 us -> 21.4 us
    pallas_call x1, Pallas kernels: 5.79 us -> 1.61 us  [fused_shards(): pl.pallas_call(functools.partial(place_kernel, T, R), out_shape=(tiles, t...]
    pallas_call x1, Pallas kernels: 20.4 us -> 19.7 us  [fused_shards(): pl.pallas_call(functools.partial(fused_kernel, T, R, H), out_shape=jax.Sh...]
where the time goes in v5:
time: 22.2 us; the launch traced here: 22 us
  Pallas kernels  21.4 us (96%)
  between operations  0.64 us (3%)
    pallas_call x1, Pallas kernels, fused_shards(): pl.pallas_call(functools.partial(fused_kernel, T, R, H), out_shape=jax.Sh...  19.7 us
    pallas_call x1, Pallas kernels, fused_shards(): pl.pallas_call(functools.partial(place_kernel, T, R), out_shape=(tiles, t...  1.61 us

profile of v5, /device:TPU:0, one launch (start us, length us, event | category | flops | bytes accessed | tf_op | source)
XLA Modules:
  0.0 22.0 jit_solution(7033116711687527620)
XLA Ops:
  0.6 19.7 %hstu_fused.1.ret_ref = bf16[64,8,128]{2,1,0:T(8,128)(2,1)} custom-call(s32[1,4,8]{2,1,0:T(4,128)} %send_ref.1, s32[1,1,8]{2,1,0:T(1,128)} %work_hbm.1, s32[1,1,4]{2,1,0:T(1,128)} %seq_hbm.1, f32[8]{0:T(128)} %slope_hbm.1, bf16[32,8,128]{2,1,0:T(8,128)(2,1)} %bitcast.4, bf16[32,8,128]{2,1,0:T(8,128)(2,1)} %bitcast.5, bf16[512,2048]{1,0:T(8,128)(2,1)} %wu_hbm.1, ...), custom_call_target="tpu_custom_call" | custom-call | tf_op jit(solution)/shard_map/hstu_fused/pallas_call | solution.py:391
  20.4 1.6 %place.1 = (bf16[32,8,128]{2,1,0:T(8,128)(2,1)}, bf16[32,8,128]{2,1,0:T(8,128)(2,1)}) custom-call(s32[1,4,8]{2,1,0:T(4,128)} %send_ref.1, bf16[64,8,128]{2,1,0:T(8,128)(2,1)} %hstu_fused.1.ret_ref), custom_call_target="tpu_custom_call" | custom-call | tf_op jit(solution)/shard_map/place/pallas_call | solution.py:433

commit v6 on v5

--- a/solution.py
+++ b/solution.py
@@ -313,6 +313,11 @@
         slopes_back.append(deriv)
     gate, value, query, key = projected
 
+    settle(cot_got, recv_sem.at[1])
+    unpack(cot_got, dy_s)
+    dy = dy_s[...]
+    dgated = mm(dy.astype(BF16), wo[...], NT).astype(BF16).astype(F32)
+
     relative = slope_s[...]
     allowed = relative >= 0.0
     weights, derivs, pieces, values, keys, queries = [], [], [], [], [], []
@@ -332,20 +337,11 @@
         values.append(vd)
         queries.append(q)
     attended, att_scale = norm_parts(jnp.concatenate(pieces, axis=1))
+    dgate = dgated * attended
+    datt = norm_back(dgated * gate, attended, att_scale).astype(BF16)
     gated = (attended * gate).astype(BF16)
     output = x + mm(gated, wo[...])
-
     scatter(output, out_back)
-    post(out_back, ret, 2)
-    out_own = pltpu.make_async_copy(out_back.at[me], ret.at[me], own_sem.at[0])
-    out_own.start()
-
-    settle(cot_got, recv_sem.at[1])
-    unpack(cot_got, dy_s)
-    dy = dy_s[...]
-    dgated = mm(dy.astype(BF16), wo[...], NT).astype(BF16).astype(F32)
-    dgate = dgated * attended
-    datt = norm_back(dgated * gate, attended, att_scale).astype(BF16)
     dv, dq, dk = [], [], []
     for g in range(H // G):
         da = datt[:, g * gw : (g + 1) * gw]
@@ -354,6 +350,9 @@
         dv.append(collect(mm(weights[g], da, TN)))
         dq.append(mm(ds, keys[g]))
         dk.append(collect(mm(ds, queries[g], TN)))
+    post(out_back, ret, 2)
+    out_own = pltpu.make_async_copy(out_back.at[me], ret.at[me], own_sem.at[0])
+    out_own.start()
     dprojected = [dgate] + [
         jnp.concatenate(parts, axis=1).astype(BF16).astype(F32) for parts in (dv, dq, dk)
     ]

time: 22.2 us -> 21.9 us (0.986)
  Pallas kernels: 21.4 us -> 21 us
    pallas_call x1, Pallas kernels: 19.7 us -> 19.4 us  [fused_shards(): pl.pallas_call(functools.partial(fused_kernel, T, R, H), out_shape=jax.Sh...]
where the time goes in v6:
time: 21.9 us; the launch traced here: 21.7 us
  Pallas kernels  21 us (96%)
  between operations  0.64 us (3%)
    pallas_call x1, Pallas kernels, fused_shards(): pl.pallas_call(functools.partial(fused_kernel, T, R, H), out_shape=jax.Sh...  19.4 us
    pallas_call x1, Pallas kernels, fused_shards(): pl.pallas_call(functools.partial(place_kernel, T, R), out_shape=(tiles, t...  1.61 us

profile of v6, /device:TPU:0, one launch (start us, length us, event | category | flops | bytes accessed | tf_op | source)
XLA Modules:
  0.0 21.7 jit_solution(2648617785509225459)
XLA Ops:
  0.6 19.4 %hstu_fused.1.ret_ref = bf16[64,8,128]{2,1,0:T(8,128)(2,1)} custom-call(s32[1,4,8]{2,1,0:T(4,128)} %send_ref.1, s32[1,1,8]{2,1,0:T(1,128)} %work_hbm.1, s32[1,1,4]{2,1,0:T(1,128)} %seq_hbm.1, f32[8]{0:T(128)} %slope_hbm.1, bf16[32,8,128]{2,1,0:T(8,128)(2,1)} %bitcast.4, bf16[32,8,128]{2,1,0:T(8,128)(2,1)} %bitcast.5, bf16[512,2048]{1,0:T(8,128)(2,1)} %wu_hbm.1, ...), custom_call_target="tpu_custom_call" | custom-call | tf_op jit(solution)/shard_map/hstu_fused/pallas_call | solution.py:390
  20.1 1.6 %place.1 = (bf16[32,8,128]{2,1,0:T(8,128)(2,1)}, bf16[32,8,128]{2,1,0:T(8,128)(2,1)}) custom-call(s32[1,4,8]{2,1,0:T(4,128)} %send_ref.1, bf16[64,8,128]{2,1,0:T(8,128)(2,1)} %hstu_fused.1.ret_ref), custom_call_target="tpu_custom_call" | custom-call | tf_op jit(solution)/shard_map/place/pallas_call | solution.py:432

commit v7 on v6

--- a/solution.py
+++ b/solution.py
@@ -214,9 +214,12 @@
             for t in range(T):
                 target[d * T + t] = source[t * R + send_ref[0, t, d]]
 
-    loads[0].wait()
-    loads[1].wait()
+    for load in loads[:3]:
+        load.wait()
+    for load in loads[6:]:
+        load.start()
     gather(emb_ref, emb_stage)
+    gather(cot_ref, cot_stage)
     pl.semaphore_wait(barrier, n - 1)
 
     def post(src, dst, index, base=0):
@@ -250,12 +253,8 @@
 
     post(emb_stage, emb_got, 0)
     emb_got[me] = emb_stage[me]
-    loads[2].wait()
-    gather(cot_ref, cot_stage)
     post(cot_stage, cot_got, 1)
     cot_got[me] = cot_stage[me]
-    for load in loads[6:]:
-        load.start()
 
     for load in loads[3:6]:
         load.wait()

time: 21.9 us -> 21.9 us (level)
  no operation moved by 1% of the time
where the time goes in v7:
time: 21.9 us; the launch traced here: 21.7 us
  Pallas kernels  21 us (96%)
  between operations  0.64 us (3%)
    pallas_call x1, Pallas kernels, fused_shards(): pl.pallas_call(functools.partial(fused_kernel, T, R, H), out_shape=jax.Sh...  19.4 us
    pallas_call x1, Pallas kernels, fused_shards(): pl.pallas_call(functools.partial(place_kernel, T, R), out_shape=(tiles, t...  1.61 us

profile of v7, /device:TPU:0, one launch (start us, length us, event | category | flops | bytes accessed | tf_op | source)
XLA Modules:
  0.0 21.7 jit_solution(10275443612838893008)
XLA Ops:
  0.6 19.4 %hstu_fused.1.ret_ref = bf16[64,8,128]{2,1,0:T(8,128)(2,1)} custom-call(s32[1,4,8]{2,1,0:T(4,128)} %send_ref.1, s32[1,1,8]{2,1,0:T(1,128)} %work_hbm.1, s32[1,1,4]{2,1,0:T(1,128)} %seq_hbm.1, f32[8]{0:T(128)} %slope_hbm.1, bf16[32,8,128]{2,1,0:T(8,128)(2,1)} %bitcast.4, bf16[32,8,128]{2,1,0:T(8,128)(2,1)} %bitcast.5, bf16[512,2048]{1,0:T(8,128)(2,1)} %wu_hbm.1, ...), custom_call_target="tpu_custom_call" | custom-call | tf_op jit(solution)/shard_map/hstu_fused/pallas_call | solution.py:389
  20.1 1.6 %place.1 = (bf16[32,8,128]{2,1,0:T(8,128)(2,1)}, bf16[32,8,128]{2,1,0:T(8,128)(2,1)}) custom-call(s32[1,4,8]{2,1,0:T(4,128)} %send_ref.1, bf16[64,8,128]{2,1,0:T(8,128)(2,1)} %hstu_fused.1.ret_ref), custom_call_target="tpu_custom_call" | custom-call | tf_op jit(solution)/shard_map/place/pallas_call | solution.py:431

commit v8 on v7

--- a/solution.py
+++ b/solution.py
@@ -312,11 +312,6 @@
         slopes_back.append(deriv)
     gate, value, query, key = projected
 
-    settle(cot_got, recv_sem.at[1])
-    unpack(cot_got, dy_s)
-    dy = dy_s[...]
-    dgated = mm(dy.astype(BF16), wo[...], NT).astype(BF16).astype(F32)
-
     relative = slope_s[...]
     allowed = relative >= 0.0
     weights, derivs, pieces, values, keys, queries = [], [], [], [], [], []
@@ -335,6 +330,10 @@
         keys.append(kd)
         values.append(vd)
         queries.append(q)
+    settle(cot_got, recv_sem.at[1])
+    unpack(cot_got, dy_s)
+    dy = dy_s[...]
+    dgated = mm(dy.astype(BF16), wo[...], NT).astype(BF16).astype(F32)
     attended, att_scale = norm_parts(jnp.concatenate(pieces, axis=1))
     dgate = dgated * attended
     datt = norm_back(dgated * gate, attended, att_scale).astype(BF16)

time: 21.9 us -> 21.6 us (0.986)
    pallas_call x1, Pallas kernels: 19.4 us -> 19.2 us  [fused_shards(): pl.pallas_call(functools.partial(fused_kernel, T, R, H), out_shape=jax.Sh...]
where the time goes in v8:
time: 21.6 us; the launch traced here: 21.4 us
  Pallas kernels  20.8 us (96%)
  between operations  0.64 us (3%)
    pallas_call x1, Pallas kernels, fused_shards(): pl.pallas_call(functools.partial(fused_kernel, T, R, H), out_shape=jax.Sh...  19.2 us
    pallas_call x1, Pallas kernels, fused_shards(): pl.pallas_call(functools.partial(place_kernel, T, R), out_shape=(tiles, t...  1.61 us

profile of v8, /device:TPU:0, one launch (start us, length us, event | category | flops | bytes accessed | tf_op | source)
XLA Modules:
  0.0 21.4 jit_solution(8430860548723674054)
XLA Ops:
  0.6 19.2 %hstu_fused.1.ret_ref = bf16[64,8,128]{2,1,0:T(8,128)(2,1)} custom-call(s32[1,4,8]{2,1,0:T(4,128)} %send_ref.1, s32[1,1,8]{2,1,0:T(1,128)} %work_hbm.1, s32[1,1,4]{2,1,0:T(1,128)} %seq_hbm.1, f32[8]{0:T(128)} %slope_hbm.1, bf16[32,8,128]{2,1,0:T(8,128)(2,1)} %bitcast.4, bf16[32,8,128]{2,1,0:T(8,128)(2,1)} %bitcast.5, bf16[512,2048]{1,0:T(8,128)(2,1)} %wu_hbm.1, ...), custom_call_target="tpu_custom_call" | custom-call | tf_op jit(solution)/shard_map/hstu_fused/pallas_call | solution.py:388
  19.8 1.6 %place.1 = (bf16[32,8,128]{2,1,0:T(8,128)(2,1)}, bf16[32,8,128]{2,1,0:T(8,128)(2,1)}) custom-call(s32[1,4,8]{2,1,0:T(4,128)} %send_ref.1, bf16[64,8,128]{2,1,0:T(8,128)(2,1)} %hstu_fused.1.ret_ref), custom_call_target="tpu_custom_call" | custom-call | tf_op jit(solution)/shard_map/place/pallas_call | solution.py:430

commit v9 on v8

--- a/solution.py
+++ b/solution.py
@@ -340,6 +340,9 @@
     gated = (attended * gate).astype(BF16)
     output = x + mm(gated, wo[...])
     scatter(output, out_back)
+    post(out_back, ret, 2)
+    out_own = pltpu.make_async_copy(out_back.at[me], ret.at[me], own_sem.at[0])
+    out_own.start()
     dv, dq, dk = [], [], []
     for g in range(H // G):
         da = datt[:, g * gw : (g + 1) * gw]
@@ -348,9 +351,6 @@
         dv.append(collect(mm(weights[g], da, TN)))
         dq.append(mm(ds, keys[g]))
         dk.append(collect(mm(ds, queries[g], TN)))
-    post(out_back, ret, 2)
-    out_own = pltpu.make_async_copy(out_back.at[me], ret.at[me], own_sem.at[0])
-    out_own.start()
     dprojected = [dgate] + [
         jnp.concatenate(parts, axis=1).astype(BF16).astype(F32) for parts in (dv, dq, dk)
     ]

time: 21.6 us -> 21.6 us (level)
  no operation moved by 1% of the time
where the time goes in v9:
time: 21.6 us; the launch traced here: 21.4 us
  Pallas kernels  20.8 us (96%)
  between operations  0.64 us (3%)
    pallas_call x1, Pallas kernels, fused_shards(): pl.pallas_call(functools.partial(fused_kernel, T, R, H), out_shape=jax.Sh...  19.2 us
    pallas_call x1, Pallas kernels, fused_shards(): pl.pallas_call(functools.partial(place_kernel, T, R), out_shape=(tiles, t...  1.61 us

profile of v9, /device:TPU:0, one launch (start us, length us, event | category | flops | bytes accessed | tf_op | source)
XLA Modules:
  0.0 21.4 jit_solution(7026162150138495668)
XLA Ops:
  0.6 19.2 %hstu_fused.1.ret_ref = bf16[64,8,128]{2,1,0:T(8,128)(2,1)} custom-call(s32[1,4,8]{2,1,0:T(4,128)} %send_ref.1, s32[1,1,8]{2,1,0:T(1,128)} %work_hbm.1, s32[1,1,4]{2,1,0:T(1,128)} %seq_hbm.1, f32[8]{0:T(128)} %slope_hbm.1, bf16[32,8,128]{2,1,0:T(8,128)(2,1)} %bitcast.4, bf16[32,8,128]{2,1,0:T(8,128)(2,1)} %bitcast.5, bf16[512,2048]{1,0:T(8,128)(2,1)} %wu_hbm.1, ...), custom_call_target="tpu_custom_call" | custom-call | tf_op jit(solution)/shard_map/hstu_fused/pallas_call | solution.py:388
  19.8 1.6 %place.1 = (bf16[32,8,128]{2,1,0:T(8,128)(2,1)}, bf16[32,8,128]{2,1,0:T(8,128)(2,1)}) custom-call(s32[1,4,8]{2,1,0:T(4,128)} %send_ref.1, bf16[64,8,128]{2,1,0:T(8,128)(2,1)} %hstu_fused.1.ret_ref), custom_call_target="tpu_custom_call" | custom-call | tf_op jit(solution)/shard_map/place/pallas_call | solution.py:430
